TPU v7x, 512 devices: a whole 4x4x16 slice. The times are simulated.
512 devices in a mesh: tract: 8 (over y, core), visit: 64 (over x, z).
Axes of the slice: x: 4, y: 4, z: 16, core: 2. Of those that a mesh axis runs over, the one named last changes fastest.
Arguments:
- images: bfloat16 [8, 2048, 6400], P('tract', 'visit'), may hold values from -6 to 6
- coefficients: bfloat16 [8, 2048, 96], P('tract', 'visit'), may hold values from -3 to 3
- orders: int32 [8, 2048], P('tract', 'visit'), may hold values from 0 to 2
- resample: bfloat16 [8, 2048, 3200], P('tract', 'visit'), may hold values from -1 to 1
- weights: bfloat16 [8, 2048], P('tract', 'visit'), may hold values from 0.049804688 to 0.5
- routes: int32 [8, 2048, 2], P('tract', 'visit'), may hold values from 0 to 63, all different within a row; in each aligned block of 32 rows (0 to 31, 32 to 63, ..., all dimensions but the last counted through in order) at most 2 rows name the same one
- offsets: int32 [8, 2048, 2, 2], P('tract', 'visit'), may hold values from 0 to 216
Outputs:
- coadd_flux: float32 [64, 256, 256], P('visit', 'tract')
- coadd_weight: float32 [64, 256, 256], P('visit', 'tract')
Inputs may be any that keep to these rules, and one draw needn't show every extreme that they name: `routes`: in the rows of one device (32 blocks, aligned), no patch is named by more than 2 pairs of block and margin; the 2 patches of a block differ.
All inputs are finite; a program needn't handle non-finite values.
Results may differ from a plain program's by a relative error of at most 0.0065.
Values may be sent and summed in bfloat16 or wider, within the bound.
No kernel may reach another device: no remote copies, remote signals or barrier semaphores. Data moves between devices by JAX's collectives and lax.ppermute only.
A program may use at most 64 MiB of HBM per device.

v0:
```python
import jax
import jax.numpy as jnp
from jax import lax
from jax.sharding import PartitionSpec as P

KSIZE = 41
NBASIS = 16
NTERMS = 6
TOP = 2
BLK = 40
PATCH = 256
HALF = 20
BLKIN = 80


SIGMAS = (0.7, 1.5, 3.0, 2.0)
POWERS = (0, 0, 0, 1)
TERM_DEGREES = (0, 1, 1, 2, 2, 2)


def kernel_tables():
    row_ids = jnp.arange(BLK, dtype=jnp.int32)[:, None]
    col_ids = jnp.arange(BLK + KSIZE - 1, dtype=jnp.int32)[None, :]
    difference = col_ids - row_ids
    inside = (difference >= 0) & (difference < KSIZE)
    shifted = difference.astype(jnp.float32) - jnp.float32(HALF)
    tap_offsets = jnp.arange(KSIZE, dtype=jnp.float32) - jnp.float32(HALF)
    tables = []
    for spread_sigma, degree_power in zip(SIGMAS, POWERS):

        def profile(offset):
            shape_value = jnp.exp(-offset * offset / (2.0 * spread_sigma * spread_sigma))
            if degree_power == 1:
                shape_value = shape_value * offset / spread_sigma
            return shape_value

        normal_sum = jnp.sum(jnp.abs(profile(tap_offsets)))
        tables.append(jnp.where(inside, profile(shifted) / normal_sum, jnp.float32(0.0)))
    return jnp.stack(tables).astype(jnp.bfloat16)


def monomial_planes():
    centres = (2.0 * jnp.arange(BLK, dtype=jnp.float32) + 1.0) / BLK - 1.0
    across = centres[:, None] * jnp.ones((1, BLK), jnp.float32)
    downward = jnp.ones((BLK, 1), jnp.float32) * centres[None, :]
    ones_plane = jnp.ones((BLK, BLK), jnp.float32)
    return jnp.stack(
        [ones_plane, across, downward, across * across, across * downward, downward * downward]
    )


def mask_coefficients(coefficients, orders):
    shaped = coefficients.reshape(orders.shape + (NBASIS, NTERMS))
    degrees = jnp.array(TERM_DEGREES, jnp.int32)
    keep = degrees <= orders[..., None, None]
    return jnp.where(keep, shaped, jnp.zeros_like(shaped))


def match_and_warp(flat_images, masked, flat_resample, tables, monomials):
    images = flat_images.reshape(-1, BLKIN, BLKIN)
    resample = flat_resample.reshape(-1, 2, BLK, BLK)
    batch_size = images.shape[0]
    accumulated = jnp.zeros((batch_size, BLK, BLK), jnp.float32)
    for row_kernel in range(4):
        smooth = jnp.einsum(
            "ix,nxy->niy", tables[row_kernel], images, preferred_element_type=jnp.float32
        ).astype(jnp.bfloat16)
        for col_kernel in range(4):
            response = jnp.einsum(
                "niy,jy->nij", smooth, tables[col_kernel], preferred_element_type=jnp.float32
            )
            factor = masked[:, 4 * row_kernel + col_kernel, :].astype(jnp.float32)
            spatial = factor[:, 0, None, None] * monomials[0]
            for monomial in range(1, NTERMS):
                spatial = spatial + factor[:, monomial, None, None] * monomials[monomial]
            accumulated = accumulated + spatial * response
    matched = accumulated.astype(jnp.bfloat16)
    halfway = jnp.einsum(
        "nij,njk->nik", resample[:, 0], matched, preferred_element_type=jnp.float32
    ).astype(jnp.bfloat16)
    return jnp.einsum(
        "nik,nlk->nil", halfway, resample[:, 1], preferred_element_type=jnp.float32
    ).astype(jnp.bfloat16)


def per_device(images, coefficients, orders, resample, weights, routes, offsets):
    tables = kernel_tables()
    monomials = monomial_planes()
    flat_images = images[0]
    flat_resample = resample[0]
    masked = mask_coefficients(coefficients[0], orders[0])
    block_count = flat_images.shape[0]
    visit_count = lax.axis_size("visit")
    capacity = max(2, 4 * block_count // visit_count)
    pair_count = block_count * TOP
    slot_count = visit_count * capacity
    destination = routes[0].reshape(pair_count)
    pair_ids = jnp.arange(pair_count, dtype=jnp.int32)
    same_patch = destination[:, None] == destination[None, :]
    earlier = pair_ids[None, :] < pair_ids[:, None]
    slot_rank = jnp.sum((same_patch & earlier).astype(jnp.int32), axis=1)
    slot_index = destination * capacity + slot_rank
    slot_pick = (jnp.arange(slot_count, dtype=jnp.int32)[:, None] == slot_index[None, :]).astype(
        jnp.bfloat16
    )
    slot_owner = (
        pair_ids[:, None] // TOP == jnp.arange(block_count, dtype=jnp.int32)[None, :]
    ).astype(jnp.bfloat16)
    choose = jnp.dot(slot_pick, slot_owner, preferred_element_type=jnp.float32).astype(jnp.bfloat16)
    pair_weight = jnp.repeat(weights[0], TOP)
    pair_offsets = offsets[0].reshape(pair_count, 2).astype(jnp.bfloat16)
    extras = jnp.concatenate([pair_offsets, pair_weight[:, None]], axis=1)
    slot_extras = jnp.dot(slot_pick, extras, preferred_element_type=jnp.float32).astype(
        jnp.bfloat16
    )
    slot_images = jnp.dot(choose, flat_images, preferred_element_type=jnp.float32).astype(
        jnp.bfloat16
    )
    slot_masked = jnp.dot(
        choose, masked.reshape(block_count, NBASIS * NTERMS), preferred_element_type=jnp.float32
    ).astype(jnp.bfloat16)
    slot_resample = jnp.dot(choose, flat_resample, preferred_element_type=jnp.float32).astype(
        jnp.bfloat16
    )
    part_images = lax.all_to_all(
        slot_images.reshape(visit_count, capacity, slot_images.shape[1]),
        "visit",
        split_axis=0,
        concat_axis=0,
        tiled=True,
    )
    part_masked = lax.all_to_all(
        slot_masked.reshape(visit_count, capacity, NBASIS * NTERMS),
        "visit",
        split_axis=0,
        concat_axis=0,
        tiled=True,
    )
    part_resample = lax.all_to_all(
        slot_resample.reshape(visit_count, capacity, slot_resample.shape[1]),
        "visit",
        split_axis=0,
        concat_axis=0,
        tiled=True,
    )
    part_extras = lax.all_to_all(
        slot_extras.reshape(visit_count, capacity, 3),
        "visit",
        split_axis=0,
        concat_axis=0,
        tiled=True,
    )
    leading = part_images.shape[:2]
    warped_here = match_and_warp(
        part_images.reshape(-1, part_images.shape[2]),
        part_masked.reshape(-1, NBASIS, NTERMS),
        part_resample.reshape(-1, part_resample.shape[2]),
        tables,
        monomials,
    )
    warped = warped_here.reshape(leading + warped_here.shape[1:])
    arrived = part_extras
    warped = warped.reshape(slot_count, BLK, BLK)
    arrived = arrived.reshape(slot_count, 3)
    pixels = jnp.arange(PATCH, dtype=jnp.float32)
    within = jnp.arange(BLK, dtype=jnp.float32)
    row_hit = (
        pixels[None, None, :]
        == arrived[:, 0, None, None].astype(jnp.float32) + within[None, :, None]
    )
    col_hit = (
        pixels[None, None, :]
        == arrived[:, 1, None, None].astype(jnp.float32) + within[None, :, None]
    )
    row_place = jnp.where(row_hit, arrived[:, 2, None, None], jnp.zeros((), jnp.bfloat16))
    col_place = col_hit.astype(jnp.bfloat16)
    spread = jnp.einsum(
        "sij,sjq->siq", warped, col_place, preferred_element_type=jnp.float32
    ).astype(jnp.bfloat16)
    coadd_flux = jnp.einsum("sip,siq->pq", row_place, spread, preferred_element_type=jnp.float32)
    row_cover = jnp.sum(row_place.astype(jnp.float32), axis=1).astype(jnp.bfloat16)
    col_cover = jnp.sum(col_place.astype(jnp.float32), axis=1).astype(jnp.bfloat16)
    coadd_weight = jnp.einsum("sp,sq->pq", row_cover, col_cover, preferred_element_type=jnp.float32)
    coadd_flux, coadd_weight = (
        lax.psum_scatter(coadd_flux, "tract", scatter_dimension=0, tiled=True),
        lax.psum_scatter(coadd_weight, "tract", scatter_dimension=0, tiled=True),
    )
    return (coadd_flux[None], coadd_weight[None])


def solution(mesh):
    in_specs = (
        P("tract", "visit", None),
        P("tract", "visit", None),
        P("tract", "visit"),
        P("tract", "visit", None),
        P("tract", "visit"),
        P("tract", "visit", None),
        P("tract", "visit", None, None),
    )
    out_specs = (P("visit", "tract", None), P("visit", "tract", None))
    return jax.shard_map(
        per_device, mesh=mesh, in_specs=in_specs, out_specs=out_specs, check_vma=False
    )
```

profile of v0, /device:TPU:1, one launch (start us, length us, event | category | flops | bytes accessed | tf_op | source)
XLA Modules:
  0.0 270.8 jit_solution(2071631069458411545)
XLA Ops:
  7.2 0.8 copy.78
  10.2 0.8 copy.108
  11.0 19.1 %all-to-all-start = ((bf16[64,2,3]{2,1,0:T(2,128)(2,1)}), bf16[64,2,3]{2,1,0:T(2,128)(2,1)S(1)}, u32[]{:S(2)}, u32[]{:S(2)}) async-start(bf16[64,2,3]{2,1,0:T(2,128)(2,1)} %bitcast.1), calls=%async_computation | async-start | bytes 65536 | tf_op jit(solution)/shard_map/all_to_all | solution.py:146
  30.3 0.8 broadcast_compare_fusion
  31.1 0.8 copy.83
  32.0 0.7 copy.84
  32.8 10.5 %all-to-all-done = bf16[64,2,3]{2,1,0:T(2,128)(2,1)S(1)} async-done(((bf16[64,2,3]{2,1,0:T(2,128)(2,1)}), bf16[64,2,3]{2,1,0:T(2,128)(2,1)S(1)}, u32[]{:S(2)}, u32[]{:S(2)}) %all-to-all-start) | async-done | bytes 800 | tf_op jit(solution)/shard_map/all_to_all | solution.py:146
  43.3 4.6 %all-to-all-start.2 = ((bf16[64,2,96]{2,1,0:T(2,128)(2,1)}), bf16[64,2,96]{2,1,0:T(2,128)(2,1)S(1)}, u32[]{:S(2)}, u32[]{:S(2)}) async-start(bf16[64,2,96]{2,1,0:T(2,128)(2,1)} %bitcast.9), calls=%async_computation.2 | async-start | bytes 65536 | tf_op jit(solution)/shard_map/all_to_all | solution.py:132
  47.9 1.3 convolution_convert_fusion.1
  49.2 1.2 reshape.454
  50.4 10.7 %all-to-all-done.2 = bf16[64,2,96]{2,1,0:T(2,128)(2,1)S(1)} async-done(((bf16[64,2,96]{2,1,0:T(2,128)(2,1)}), bf16[64,2,96]{2,1,0:T(2,128)(2,1)S(1)}, u32[]{:S(2)}, u32[]{:S(2)}) %all-to-all-start.2) | async-done | bytes 24608 | tf_op jit(solution)/shard_map/all_to_all | solution.py:132
  61.1 4.6 %all-to-all-start.1 = ((bf16[64,2,3200]{2,1,0:T(2,128)(2,1)}), bf16[64,2,3200]{2,1,0:T(2,128)(2,1)S(1)}, u32[]{:S(2)}, u32[]{:S(2)}) async-start(bf16[64,2,3200]{2,1,0:T(2,128)(2,1)} %reshape.454), calls=%async_computation.1 | async-start | bytes 1638400 | tf_op jit(solution)/shard_map/all_to_all | solution.py:139
  66.4 1.6 reshape.457
  67.9 36.7 %all-to-all-done.1 = bf16[64,2,3200]{2,1,0:T(2,128)(2,1)S(1)} async-done(((bf16[64,2,3200]{2,1,0:T(2,128)(2,1)}), bf16[64,2,3200]{2,1,0:T(2,128)(2,1)S(1)}, u32[]{:S(2)}, u32[]{:S(2)}) %all-to-all-start.1) | async-done | bytes 819232 | tf_op jit(solution)/shard_map/all_to_all | solution.py:139
  104.7 10.4 %all-to-all-start.3 = ((bf16[64,2,6400]{2,1,0:T(2,128)(2,1)}), bf16[64,2,6400]{2,1,0:T(2,128)(2,1)S(1)}, u32[]{:S(2)}, u32[]{:S(2)}) async-start(bf16[64,2,6400]{2,1,0:T(2,128)(2,1)} %reshape.457), calls=%async_computation.3 | async-start | bytes 3276800 | tf_op jit(solution)/shard_map/all_to_all | solution.py:125
  118.2 0.9 fusion.6
  119.7 0.9 fusion.201
  121.4 1.0 slice_convert_fusion
  127.0 0.9 slice_reduce_fusion.5
  127.9 5.3 %reshape_reshape.6 = bf16[128,2,40,40]{3,2,1,0:T(8,128)(2,1)} reshape(bf16[64,2,3200]{2,1,0:T(2,128)(2,1)S(1)} %all-to-all-done.1) | data formatting | bytes 1638400 | tf_op jit(solution)/shard_map/reshape;reshape | solution.py:61
  133.2 54.2 %all-to-all-done.3 = bf16[64,2,6400]{2,1,0:T(2,128)(2,1)S(1)} async-done(((bf16[64,2,6400]{2,1,0:T(2,128)(2,1)}), bf16[64,2,6400]{2,1,0:T(2,128)(2,1)S(1)}, u32[]{:S(2)}, u32[]{:S(2)}) %all-to-all-start.3) | async-done | bytes 1638432 | tf_op jit(solution)/shard_map/all_to_all | solution.py:125
  187.4 4.3 %reshape_reshape.7 = bf16[128,80,80]{2,1,0:T(8,128)(2,1)} reshape(bf16[64,2,6400]{2,1,0:T(2,128)(2,1)S(1)} %all-to-all-done.3) | data formatting | bytes 3276800 | tf_op jit(solution)/shard_map/reshape;reshape | solution.py:60
  191.7 4.3 %copy.85 = bf16[128,80,80]{0,1,2:T(8,128)(2,1)S(1)} copy(bf16[128,80,80]{2,1,0:T(8,128)(2,1)} %reshape_reshape.7) | data formatting | bytes 3276800 | tf_op jit(solution)/shard_map/reshape;reshape | solution.py:60
  195.9 1.0 fusion.13
  197.0 1.0 fusion.14
  198.0 1.0 fusion.15
  199.0 0.9 fusion.16
  199.9 1.0 convolution_multiply_fusion.15
  200.9 1.0 fusion.31
  202.0 1.0 fusion.30
  203.0 0.9 fusion.29
  203.9 1.0 fusion.28
  205.0 1.0 fusion.27
  206.0 1.0 fusion.26
  207.1 0.9 fusion.25
  208.0 1.0 fusion.24
  209.1 1.0 fusion.23
  210.1 1.0 fusion.22
  211.1 0.9 fusion.21
  212.1 1.0 fusion.20
  213.1 1.0 fusion.19
  214.2 1.0 fusion.18
  215.3 1.9 fusion.32
  217.2 2.0 copy.105
  219.2 3.9 %convolution_convert_fusion.2 = bf16[128,40,40]{2,1,0:T(8,128)(2,1)} fusion(bf16[128,40,40]{2,1,0:T(8,128)(2,1)} %copy.105, bf16[128,2,40,40]{3,2,1,0:T(8,128)(2,1)S(1)} %copy-done.1), kind=kOutput, calls=%fused_computation.14 | convolution fusion | flops 33177600 | bytes 1638400 | tf_op jit(solution)/shard_map/nik,nlk->nil/dot_general | solution.py:81
  223.1 2.7 fusion.10
  225.8 1.6 fusion.33
  227.4 36.6 %reduce-scatter.3.cloned.1.call-done = f32[32,256]{1,0:T(8,128)} async-done(((f32[256,256]{1,0:T(8,128)}), f32[32,256]{1,0:T(8,128)}) %reduce-scatter.3.cloned.1.call-update) | async-done | bytes 32784 | tf_op jit(solution)/shard_map/reduce_scatter | solution.py:185
  (68 shorter events, 12.4 us)
Async XLA Ops:
  7.2 58.6 %copy-start = (bf16[1,32,6400]{2,1,0:T(8,128)(2,1)S(1)}, bf16[1,32,6400]{2,1,0:T(8,128)(2,1)}, u32[]{:S(2)}) copy-start(bf16[1,32,6400]{2,1,0:T(8,128)(2,1)} %param.8) | copy-start | bytes 1228804
  11.0 32.3 %all-to-all-start = ((bf16[64,2,3]{2,1,0:T(2,128)(2,1)}), bf16[64,2,3]{2,1,0:T(2,128)(2,1)S(1)}, u32[]{:S(2)}, u32[]{:S(2)}) async-start(bf16[64,2,3]{2,1,0:T(2,128)(2,1)} %bitcast.1), calls=%async_computation | async-start | bytes 65536 | tf_op jit(solution)/shard_map/all_to_all | solution.py:146
  43.3 17.8 %all-to-all-start.2 = ((bf16[64,2,96]{2,1,0:T(2,128)(2,1)}), bf16[64,2,96]{2,1,0:T(2,128)(2,1)S(1)}, u32[]{:S(2)}, u32[]{:S(2)}) async-start(bf16[64,2,96]{2,1,0:T(2,128)(2,1)} %bitcast.9), calls=%async_computation.2 | async-start | bytes 65536 | tf_op jit(solution)/shard_map/all_to_all | solution.py:132
  61.1 43.6 %all-to-all-start.1 = ((bf16[64,2,3200]{2,1,0:T(2,128)(2,1)}), bf16[64,2,3200]{2,1,0:T(2,128)(2,1)S(1)}, u32[]{:S(2)}, u32[]{:S(2)}) async-start(bf16[64,2,3200]{2,1,0:T(2,128)(2,1)} %reshape.454), calls=%async_computation.1 | async-start | bytes 1638400 | tf_op jit(solution)/shard_map/all_to_all | solution.py:139
  104.7 82.7 %all-to-all-start.3 = ((bf16[64,2,6400]{2,1,0:T(2,128)(2,1)}), bf16[64,2,6400]{2,1,0:T(2,128)(2,1)S(1)}, u32[]{:S(2)}, u32[]{:S(2)}) async-start(bf16[64,2,6400]{2,1,0:T(2,128)(2,1)} %reshape.457), calls=%async_computation.3 | async-start | bytes 3276800 | tf_op jit(solution)/shard_map/all_to_all | solution.py:125
  115.1 112.3 %reduce-scatter.5.cloned.1.call-start = ((), (), s32[]{:S(2)}) async-start(), calls=%async_computation.7 | async-start | bytes 294912 | tf_op jit(solution)/shard_map/reduce_scatter | solution.py:186
  117.7 96.5 %copy-start.8 = (f32[40]{0:T(128)}, f32[40]{0:T(128)S(1)}, u32[]{:S(2)}) copy-start(f32[40]{0:T(128)S(1)} %get-tuple-element.120) | copy-start | bytes 484
  120.6 143.4 %reduce-scatter.3.cloned.1.call-start = ((), (), s32[]{:S(2)}) async-start(), calls=%async_computation.6 | async-start | bytes 294912 | tf_op jit(solution)/shard_map/reduce_scatter | solution.py:185
  214.2 1.1 copy-start.2
  214.2 1.1 copy-start.3
  214.2 1.1 copy-start.4
  214.2 1.1 copy-start.5
  214.2 1.1 copy-start.6
  214.2 1.1 copy-start.7
  215.3 3.9 %copy-start.1 = (bf16[128,2,40,40]{3,2,1,0:T(8,128)(2,1)S(1)}, bf16[128,2,40,40]{3,2,1,0:T(8,128)(2,1)}, u32[]{:S(2)}) copy-start(bf16[128,2,40,40]{3,2,1,0:T(8,128)(2,1)} %reshape_reshape.6) | copy-start | bytes 2457604
Sparse Core Ops, SparseCore 0:
  120.7 39.9 reduce-scatter.4
  227.5 36.4 reduce-scatter.2
where the time goes:
time: 272 us; the launch traced here: 271 us
  waiting for transfers between devices  149 us (55%)
  starting transfers between devices  39 us (14%)
  matrix products  32.4 us (12%)
  local copies, waits for them, and re-layouts  29.4 us (11%)
  between operations  14.5 us (5%)
  other arithmetic  6.77 us (2%)
    all_to_all x1, waiting for transfers between devices, per_device(): lax.all_to_all(slot_images.reshape(visit_count, capacity, slot_images.sha...  54.2 us
    all_to_all x1, waiting for transfers between devices, per_device(): lax.all_to_all(slot_resample.reshape(visit_count, capacity, slot_resample...  36.7 us
    reduce_scatter x1, waiting for transfers between devices, per_device(): lax.psum_scatter(coadd_flux, 'tract', scatter_dimension=0, tiled=True)  36.6 us
    all_to_all x1, starting transfers between devices, per_device(): lax.all_to_all(slot_extras.reshape(visit_count, capacity, 3), 'visit', sp...  19.1 us
    dot_general x16, matrix products, match_and_warp(): jnp.einsum('niy,jy->nij', smooth, tables[col_kernel], preferred_element_t...  17 us
    all_to_all x1, waiting for transfers between devices, per_device(): lax.all_to_all(slot_masked.reshape(visit_count, capacity, NBASIS * NTERMS...  10.7 us
    all_to_all x1, waiting for transfers between devices, per_device(): lax.all_to_all(slot_extras.reshape(visit_count, capacity, 3), 'visit', sp...  10.5 us
    all_to_all x1, starting transfers between devices, per_device(): lax.all_to_all(slot_images.reshape(visit_count, capacity, slot_images.sha...  10.4 us
  transfers between devices with their start and end apart: 6, of which 5 were waited for; matrix products, arithmetic and copies ran while one was open for 24% of the time, Pallas kernels for 0%

commit v1 on v0

--- a/solution.py
+++ b/solution.py
@@ -83,17 +83,20 @@
     ).astype(jnp.bfloat16)
 
 
+WIDTH = 1664
+
+
 def per_device(images, coefficients, orders, resample, weights, routes, offsets):
     tables = kernel_tables()
     monomials = monomial_planes()
-    flat_images = images[0]
-    flat_resample = resample[0]
     masked = mask_coefficients(coefficients[0], orders[0])
-    block_count = flat_images.shape[0]
+    block_count = images.shape[1]
     visit_count = lax.axis_size("visit")
+    tract_count = lax.axis_size("tract")
     capacity = max(2, 4 * block_count // visit_count)
     pair_count = block_count * TOP
     slot_count = visit_count * capacity
+    warped_here = match_and_warp(images[0], masked, resample[0], tables, monomials)
     destination = routes[0].reshape(pair_count)
     pair_ids = jnp.arange(pair_count, dtype=jnp.int32)
     same_patch = destination[:, None] == destination[None, :]
@@ -113,55 +116,16 @@
     slot_extras = jnp.dot(slot_pick, extras, preferred_element_type=jnp.float32).astype(
         jnp.bfloat16
     )
-    slot_images = jnp.dot(choose, flat_images, preferred_element_type=jnp.float32).astype(
-        jnp.bfloat16
-    )
-    slot_masked = jnp.dot(
-        choose, masked.reshape(block_count, NBASIS * NTERMS), preferred_element_type=jnp.float32
+    slot_warped = jnp.dot(
+        choose, warped_here.reshape(block_count, BLK * BLK), preferred_element_type=jnp.float32
     ).astype(jnp.bfloat16)
-    slot_resample = jnp.dot(choose, flat_resample, preferred_element_type=jnp.float32).astype(
-        jnp.bfloat16
-    )
-    part_images = lax.all_to_all(
-        slot_images.reshape(visit_count, capacity, slot_images.shape[1]),
-        "visit",
-        split_axis=0,
-        concat_axis=0,
-        tiled=True,
-    )
-    part_masked = lax.all_to_all(
-        slot_masked.reshape(visit_count, capacity, NBASIS * NTERMS),
-        "visit",
-        split_axis=0,
-        concat_axis=0,
-        tiled=True,
-    )
-    part_resample = lax.all_to_all(
-        slot_resample.reshape(visit_count, capacity, slot_resample.shape[1]),
-        "visit",
-        split_axis=0,
-        concat_axis=0,
-        tiled=True,
-    )
-    part_extras = lax.all_to_all(
-        slot_extras.reshape(visit_count, capacity, 3),
-        "visit",
-        split_axis=0,
-        concat_axis=0,
-        tiled=True,
-    )
-    leading = part_images.shape[:2]
-    warped_here = match_and_warp(
-        part_images.reshape(-1, part_images.shape[2]),
-        part_masked.reshape(-1, NBASIS, NTERMS),
-        part_resample.reshape(-1, part_resample.shape[2]),
-        tables,
-        monomials,
-    )
-    warped = warped_here.reshape(leading + warped_here.shape[1:])
-    arrived = part_extras
-    warped = warped.reshape(slot_count, BLK, BLK)
-    arrived = arrived.reshape(slot_count, 3)
+    parcel = jnp.concatenate([slot_warped, slot_extras], axis=1)
+    parcel = jnp.pad(parcel, ((0, 0), (0, WIDTH - parcel.shape[1])))
+    parcel = lax.all_to_all(
+        parcel.reshape(visit_count, capacity, WIDTH), "visit", split_axis=0, concat_axis=0, tiled=True
+    ).reshape(slot_count, WIDTH)
+    warped = parcel[:, : BLK * BLK].reshape(slot_count, BLK, BLK)
+    arrived = parcel[:, BLK * BLK : BLK * BLK + 3]
     pixels = jnp.arange(PATCH, dtype=jnp.float32)
     within = jnp.arange(BLK, dtype=jnp.float32)
     row_hit = (
@@ -177,15 +141,20 @@
     spread = jnp.einsum(
         "sij,sjq->siq", warped, col_place, preferred_element_type=jnp.float32
     ).astype(jnp.bfloat16)
-    coadd_flux = jnp.einsum("sip,siq->pq", row_place, spread, preferred_element_type=jnp.float32)
+    partial = jnp.einsum("sip,siq->pq", row_place, spread, preferred_element_type=jnp.float32)
     row_cover = jnp.sum(row_place.astype(jnp.float32), axis=1).astype(jnp.bfloat16)
     col_cover = jnp.sum(col_place.astype(jnp.float32), axis=1).astype(jnp.bfloat16)
-    coadd_weight = jnp.einsum("sp,sq->pq", row_cover, col_cover, preferred_element_type=jnp.float32)
-    coadd_flux, coadd_weight = (
-        lax.psum_scatter(coadd_flux, "tract", scatter_dimension=0, tiled=True),
-        lax.psum_scatter(coadd_weight, "tract", scatter_dimension=0, tiled=True),
+    partial_weight = jnp.einsum(
+        "sp,sq->pq", row_cover, col_cover, preferred_element_type=jnp.float32
     )
-    return (coadd_flux[None], coadd_weight[None])
+    rows = PATCH // tract_count
+    both = jnp.concatenate(
+        [partial.reshape(tract_count, rows, PATCH), partial_weight.reshape(tract_count, rows, PATCH)],
+        axis=1,
+    ).astype(jnp.bfloat16)
+    both = lax.all_to_all(both, "tract", split_axis=0, concat_axis=0, tiled=True)
+    sums = jnp.sum(both.astype(jnp.float32), axis=0)
+    return (sums[None, :rows], sums[None, rows:])
 
 
 def solution(mesh):

time: 272 us -> 98.3 us (0.36)
  waiting for transfers between devices: 149 us -> 0 us
  blocking collectives: 0 us -> 58.3 us
  starting transfers between devices: 39 us -> 0 us
  local copies, waits for them, and re-layouts: 29.4 us -> 9.25 us
  between operations: 14.5 us -> 0.99 us
  matrix products: 32.4 us -> 23.3 us
    all_to_all x4 -> x0, waiting for transfers between devices: 112 us -> none  [the longest x1 54.2 us: per_device(): lax.all_to_all(slot_images.reshape(visit_count, capacity, slot_images.sha...]
    all_to_all x0 -> x2, blocking collectives: none -> 58.3 us  [the longest x1 44 us: per_device(): lax.all_to_all(parcel.reshape(visit_count, capacity, WIDTH), 'visit', spl...]
    all_to_all x4 -> x0, starting transfers between devices: 38.8 us -> none  [the longest x1 19.1 us: per_device(): lax.all_to_all(slot_extras.reshape(visit_count, capacity, 3), 'visit', sp...]
    reduce_scatter x2 -> x0, waiting for transfers between devices: 36.6 us -> none  [the longest x1 36.6 us: per_device(): lax.psum_scatter(coadd_flux, 'tract', scatter_dimension=0, tiled=True)]
    another operation x2 -> x1, local copies, waits for them, and re-layouts: 8.58 us -> 2.07 us  [match_and_warp(): images = flat_images.reshape(-1, BLKIN, BLKIN)]
    slice x16 -> x1, local copies, waits for them, and re-layouts: 5.47 us -> 0.24 us  [per_device(): warped = parcel[:, :BLK * BLK].reshape(slot_count, BLK, BLK)]
    another operation x1, local copies, waits for them, and re-layouts: 5.25 us -> 0.96 us  [match_and_warp(): resample = flat_resample.reshape(-1, 2, BLK, BLK)]
    dot_general x1, matrix products: 3.9 us -> 0.58 us  [match_and_warp(): jnp.einsum('nik,nlk->nil', halfway, resample[:, 1], preferred_element_typ...]
  transfers between devices with their start and end apart: 6 -> 0, of which waited for: 5 -> 0; matrix products, arithmetic and copies ran while one was open for 24% -> 0% of each run, Pallas kernels for 0% -> 0%
where the time goes in v1:
time: 98.3 us; the launch traced here: 97.9 us
  blocking collectives  58.3 us (59%)
  matrix products  23.3 us (24%)
  local copies, waits for them, and re-layouts  9.25 us (9%)
  other arithmetic  6.09 us (6%)
  between operations  0.99 us (1%)
    all_to_all x1, blocking collectives, per_device(): lax.all_to_all(parcel.reshape(visit_count, capacity, WIDTH), 'visit', spl...  44 us
    dot_general x16, matrix products, match_and_warp(): jnp.einsum('niy,jy->nij', smooth, tables[col_kernel], preferred_element_t...  15.9 us
    all_to_all x1, blocking collectives, per_device(): lax.all_to_all(both, 'tract', split_axis=0, concat_axis=0, tiled=True)  14.3 us
    dot_general x4, matrix products, match_and_warp(): jnp.einsum('ix,nxy->niy', tables[row_kernel], images, preferred_element_t...  3.52 us
    reduce_sum x4, other arithmetic, kernel_tables(): normal_sum = jnp.sum(jnp.abs(profile(tap_offsets)))  2.55 us
    another operation x1, local copies, waits for them, and re-layouts, match_and_warp(): images = flat_images.reshape(-1, BLKIN, BLKIN)  2.07 us

profile of v1, /device:TPU:1, one launch (start us, length us, event | category | flops | bytes accessed | tf_op | source)
XLA Modules:
  0.0 97.9 jit_solution(737496888034069478)
XLA Ops:
  0.6 0.6 exponential_reduce_fusion.2
  1.2 0.6 exponential_reduce_fusion.1
  1.9 0.7 exponential_reduce_fusion
  2.6 0.6 abs_reduce_fusion
  3.2 0.7 convert_element_type.264
  3.9 0.7 broadcast_in_dim.59
  4.9 0.8 copy.29
  5.8 0.2 convert_reduce_fusion.3
  6.1 0.8 copy.30
  7.0 0.7 broadcast_compare_fusion
  7.7 2.1 %reshape_squeeze.15 = bf16[32,80,80]{2,1,0:T(8,128)(2,1)S(1)} reshape(bf16[1,32,6400]{2,1,0:T(8,128)(2,1)} %param.8) | data formatting | bytes 819200 | tf_op jit(solution)/shard_map/reshape;squeeze | solution.py:60
  9.8 0.8 fusion.32
  10.6 0.9 fusion.31
  11.6 0.9 fusion.30
  12.5 0.9 fusion.29
  13.4 1.0 reshape_squeeze.16
  14.5 1.0 convolution_multiply_fusion.15
  15.5 1.0 %fusion.27 = f32[32,40,40]{2,1,0:T(8,128)S(1)} fusion(f32[32,40,40]{2,1,0:T(8,128)S(1)} %convolution_multiply_fusion.15, bf16[32,40,80]{2,1,0:T(8,128)(2,1)S(1)} %fusion.29, f32[32]{0:T(128)S(1)} %get-tuple-element.107, f32[32]{0:T(128)S(1)} %get-tuple-element.108, f32[32]{0:T(128)S(1)} %get-tuple-element.109, f32[32]{0:T(128)S(1)} %get-tuple-element.110, ...), kind=kOutput, calls=%fused_computation.44 | convolution fusion | flops 8844800 | bytes 621892 | tf_op jit(solution)/shard_map/niy,jy->nij/dot_general | solution.py:69
  16.5 1.1 %fusion.26 = f32[32,40,40]{2,1,0:T(8,128)S(1)} fusion(f32[32,40,40]{2,1,0:T(8,128)S(1)} %fusion.27, bf16[32,40,80]{2,1,0:T(8,128)(2,1)S(1)} %fusion.29, f32[32]{0:T(128)S(1)} %get-tuple-element.158, f32[32]{0:T(128)S(1)} %get-tuple-element.157, f32[32]{0:T(128)S(1)} %get-tuple-element.156, f32[32]{0:T(128)S(1)} %get-tuple-element.155, ...), kind=kOutput, calls=%fused_computation.42 | convolution fusion | flops 8844800 | bytes 621892 | tf_op jit(solution)/shard_map/niy,jy->nij/dot_general | solution.py:69
  17.5 0.9 fusion.25
  18.5 1.0 %fusion.24 = f32[32,40,40]{2,1,0:T(8,128)S(1)} fusion(f32[32,40,40]{2,1,0:T(8,128)S(1)} %fusion.25, bf16[32,40,80]{2,1,0:T(8,128)(2,1)S(1)} %fusion.30, f32[32]{0:T(128)S(1)} %get-tuple-element.152, f32[32]{0:T(128)S(1)} %get-tuple-element.151, f32[32]{0:T(128)S(1)} %get-tuple-element.150, f32[32]{0:T(128)S(1)} %get-tuple-element.149, ...), kind=kOutput, calls=%fused_computation.38 | convolution fusion | flops 8844800 | bytes 621892 | tf_op jit(solution)/shard_map/niy,jy->nij/dot_general | solution.py:69
  19.5 1.0 %fusion.23 = f32[32,40,40]{2,1,0:T(8,128)S(1)} fusion(f32[32,40,40]{2,1,0:T(8,128)S(1)} %fusion.24, bf16[32,40,80]{2,1,0:T(8,128)(2,1)S(1)} %fusion.30, f32[32]{0:T(128)S(1)} %get-tuple-element.83, f32[32]{0:T(128)S(1)} %get-tuple-element.84, f32[32]{0:T(128)S(1)} %get-tuple-element.85, f32[32]{0:T(128)S(1)} %get-tuple-element.86, ...), kind=kOutput, calls=%fused_computation.36 | convolution fusion | flops 8844800 | bytes 621892 | tf_op jit(solution)/shard_map/niy,jy->nij/dot_general | solution.py:69
  20.5 1.0 %fusion.22 = f32[32,40,40]{2,1,0:T(8,128)S(1)} fusion(f32[32,40,40]{2,1,0:T(8,128)S(1)} %fusion.23, bf16[32,40,80]{2,1,0:T(8,128)(2,1)S(1)} %fusion.30, f32[32]{0:T(128)S(1)} %get-tuple-element.146, f32[32]{0:T(128)S(1)} %get-tuple-element.145, f32[32]{0:T(128)S(1)} %get-tuple-element.144, f32[32]{0:T(128)S(1)} %get-tuple-element.143, ...), kind=kOutput, calls=%fused_computation.34 | convolution fusion | flops 8844800 | bytes 621892 | tf_op jit(solution)/shard_map/niy,jy->nij/dot_general | solution.py:69
  21.5 0.9 fusion.21
  22.5 1.0 %fusion.20 = f32[32,40,40]{2,1,0:T(8,128)S(1)} fusion(f32[32,40,40]{2,1,0:T(8,128)S(1)} %fusion.21, bf16[32,40,80]{2,1,0:T(8,128)(2,1)S(1)} %fusion.31, f32[32]{0:T(128)S(1)} %get-tuple-element.140, f32[32]{0:T(128)S(1)} %get-tuple-element.139, f32[32]{0:T(128)S(1)} %get-tuple-element.138, f32[32]{0:T(128)S(1)} %get-tuple-element.137, ...), kind=kOutput, calls=%fused_computation.30 | convolution fusion | flops 8844800 | bytes 621892 | tf_op jit(solution)/shard_map/niy,jy->nij/dot_general | solution.py:69
  23.5 1.0 %fusion.19 = f32[32,40,40]{2,1,0:T(8,128)S(1)} fusion(f32[32,40,40]{2,1,0:T(8,128)S(1)} %fusion.20, bf16[32,40,80]{2,1,0:T(8,128)(2,1)S(1)} %fusion.31, f32[32]{0:T(128)S(1)} %get-tuple-element.59, f32[32]{0:T(128)S(1)} %get-tuple-element.60, f32[32]{0:T(128)S(1)} %get-tuple-element.61, f32[32]{0:T(128)S(1)} %get-tuple-element.62, ...), kind=kOutput, calls=%fused_computation.28 | convolution fusion | flops 8844800 | bytes 621892 | tf_op jit(solution)/shard_map/niy,jy->nij/dot_general | solution.py:69
  24.5 1.0 %fusion.18 = f32[32,40,40]{2,1,0:T(8,128)S(1)} fusion(f32[32,40,40]{2,1,0:T(8,128)S(1)} %fusion.19, bf16[32,40,80]{2,1,0:T(8,128)(2,1)S(1)} %fusion.31, f32[32]{0:T(128)S(1)} %get-tuple-element.134, f32[32]{0:T(128)S(1)} %get-tuple-element.133, f32[32]{0:T(128)S(1)} %get-tuple-element.132, f32[32]{0:T(128)S(1)} %get-tuple-element.131, ...), kind=kOutput, calls=%fused_computation.26 | convolution fusion | flops 8844800 | bytes 621892 | tf_op jit(solution)/shard_map/niy,jy->nij/dot_general | solution.py:69
  25.5 0.9 fusion.17
  26.4 1.0 %fusion.16 = f32[32,40,40]{2,1,0:T(8,128)S(1)} fusion(f32[32,40,40]{2,1,0:T(8,128)S(1)} %fusion.17, bf16[32,40,80]{2,1,0:T(8,128)(2,1)S(1)} %fusion.32, f32[32]{0:T(128)S(1)} %get-tuple-element.128, f32[32]{0:T(128)S(1)} %get-tuple-element.127, f32[32]{0:T(128)S(1)} %get-tuple-element.126, f32[32]{0:T(128)S(1)} %get-tuple-element.125, ...), kind=kOutput, calls=%fused_computation.22 | convolution fusion | flops 8844800 | bytes 621892 | tf_op jit(solution)/shard_map/niy,jy->nij/dot_general | solution.py:69
  27.5 1.0 %fusion.15 = f32[32,40,40]{2,1,0:T(8,128)S(1)} fusion(f32[32,40,40]{2,1,0:T(8,128)S(1)} %fusion.16, bf16[32,40,80]{2,1,0:T(8,128)(2,1)S(1)} %fusion.32, f32[32]{0:T(128)S(1)} %get-tuple-element.35, f32[32]{0:T(128)S(1)} %get-tuple-element.36, f32[32]{0:T(128)S(1)} %get-tuple-element.37, f32[32]{0:T(128)S(1)} %get-tuple-element.38, ...), kind=kOutput, calls=%fused_computation.20 | convolution fusion | flops 8844800 | bytes 621892 | tf_op jit(solution)/shard_map/niy,jy->nij/dot_general | solution.py:69
  28.5 1.0 %fusion.14 = f32[32,40,40]{2,1,0:T(8,128)S(1)} fusion(f32[32,40,40]{2,1,0:T(8,128)S(1)} %fusion.15, bf16[32,40,80]{2,1,0:T(8,128)(2,1)S(1)} %fusion.32, f32[32]{0:T(128)S(1)} %get-tuple-element.122, f32[32]{0:T(128)S(1)} %get-tuple-element.121, f32[32]{0:T(128)S(1)} %get-tuple-element.120, f32[32]{0:T(128)S(1)} %get-tuple-element.119, ...), kind=kOutput, calls=%fused_computation.18 | convolution fusion | flops 8844800 | bytes 621892 | tf_op jit(solution)/shard_map/niy,jy->nij/dot_general | solution.py:69
  29.5 0.9 fusion.28
  30.4 0.6 convolution_convert_fusion.5
  31.0 0.2 reshape.449
  31.4 0.5 convolution_convert_fusion
  32.0 0.3 copy.44
  32.4 44.0 %all_to_all.10 = bf16[64,2,1664]{2,1,0:T(2,128)(2,1)S(1)} all-to-all(bf16[64,2,1664]{2,1,0:T(2,128)(2,1)S(1)} %reshape.450), channel_id=1, replica_groups=mesh['tract'=8,'visit'=64] {'visit'}, dimensions={0} | all-to-all | bytes 851968 | tf_op jit(solution)/shard_map/all_to_all | solution.py:124
  76.6 0.2 slice_reduce_fusion
  76.8 0.2 convert_reduce_fusion.1
  77.0 0.9 fusion.6
  77.9 0.2 copy.37
  78.2 1.5 %copy.38 = bf16[128,40,40]{2,1,0:T(8,128)(2,1)S(1)} copy(bf16[128,40,40]{0,2,1:T(8,128)(2,1)S(1)} %bitcast.373) | data formatting | bytes 819200 | tf_op jit(solution)/shard_map/reshape | solution.py:127
  79.7 1.6 %fusion.10 = bf16[128,40,256]{2,1,0:T(8,128)(2,1)S(1)} fusion(bf16[128,40,40]{2,1,0:T(8,128)(2,1)S(1)} %copy.38, f32[128,40]{1,0:T(8,128)S(1)} %iota_add_fusion), kind=kOutput, calls=%fused_computation.12 | convolution fusion | flops 107479040 | bytes 3051520 | tf_op jit(solution)/shard_map/sij,sjq->siq/dot_general | solution.py:141
  81.2 0.6 fusion.3
  81.8 0.9 fusion.38
  82.7 0.2 convolution_convert_fusion.7
  82.9 14.3 %all_to_all.11 = bf16[8,64,256]{2,1,0:T(8,128)(2,1)S(1)} all-to-all(bf16[8,64,256]{2,1,0:T(8,128)(2,1)S(1)} %pad_maximum_fusion.1), channel_id=1, replica_groups=mesh['tract'=8,'visit'=64] {'tract'}, dimensions={0} | all-to-all | bytes 524288 | tf_op jit(solution)/shard_map/all_to_all | solution.py:155
  97.2 0.6 slice_bitcast_fusion.5
  (29 shorter events, 1.3 us)
Async XLA Ops:
  6.1 7.3 %copy-start = (bf16[1,32,3200]{2,1,0:T(8,128)(2,1)S(1)}, bf16[1,32,3200]{2,1,0:T(8,128)(2,1)}, u32[]{:S(2)}) copy-start(bf16[1,32,3200]{2,1,0:T(8,128)(2,1)} %param.11) | copy-start | bytes 614404

commit v2 on v1

v2 whole, which is shorter than its diff:
```python
import functools

import jax
import jax.numpy as jnp
import numpy as np
from jax import lax
from jax.experimental import pallas as pl
from jax.experimental.pallas import tpu as pltpu
from jax.sharding import PartitionSpec as P

KSIZE = 41
NBASIS = 16
NTERMS = 6
TOP = 2
BLK = 40
PATCH = 256
HALF = 20
BLKIN = 80
LANES = 128
WIDTH = 1664
EXTRA = 1600 % LANES

SIGMAS = (0.7, 1.5, 3.0, 2.0)
POWERS = (0, 0, 0, 1)
COLUMN_AT = (0, 40, 80, 128)


def constant_tables():
    difference = np.arange(BLKIN)[None, :] - np.arange(BLK)[:, None]
    inside = (difference >= 0) & (difference < KSIZE)
    shifted = (difference - HALF).astype(np.float32)
    taps = np.arange(KSIZE, dtype=np.float32) - np.float32(HALF)
    tables = []
    for sigma, power in zip(SIGMAS, POWERS):

        def profile(offset):
            value = np.exp(-offset * offset / np.float32(2.0 * sigma * sigma)).astype(np.float32)
            if power == 1:
                value = value * offset / np.float32(sigma)
            return value.astype(np.float32)

        total = np.sum(np.abs(profile(taps)), dtype=np.float32)
        tables.append(np.where(inside, profile(shifted) / total, np.float32(0.0)))
    centres = ((2.0 * np.arange(BLK, dtype=np.float32) + 1.0) / BLK - 1.0).astype(np.float32)
    row_tables = np.concatenate(tables, axis=0)
    column_tables = np.zeros((LANES, 2 * LANES), np.float32)
    spread = np.zeros((4 * NTERMS, NTERMS, 2 * LANES), np.float32)
    across = np.zeros((8, 2 * LANES), np.float32)
    for c, at in enumerate(COLUMN_AT):
        column_tables[:BLKIN, at : at + BLK] = tables[c].T
        across[:, at : at + BLK] = centres
        for m in range(NTERMS):
            spread[c * NTERMS + m, m, at : at + BLK] = 1.0
    return (
        jnp.asarray(row_tables, jnp.bfloat16),
        jnp.asarray(column_tables, jnp.bfloat16),
        jnp.asarray(spread.reshape(4 * NTERMS, NTERMS * 2 * LANES), jnp.bfloat16),
        jnp.asarray(across),
    )


def warp_kernel(
    images_ref,
    coefficients_ref,
    orders_ref,
    resample_ref,
    weights_ref,
    routes_ref,
    offsets_ref,
    row_tables_ref,
    column_tables_ref,
    spread_ref,
    across_ref,
    out_ref,
    image_rows,
    resample_rows,
    planes,
    warped_rows,
    flat,
):
    f32, bf16 = jnp.float32, jnp.bfloat16
    blocks = images_ref.shape[0]
    group = 4
    wide = 2 * LANES

    for x in range(BLKIN):
        start = min(x * BLKIN, BLKIN * BLKIN - LANES)
        piece = images_ref[:, start : start + LANES].astype(f32)
        if start != x * BLKIN:
            piece = jnp.roll(piece, start - x * BLKIN, axis=1)
        image_rows[pl.ds(x, blocks, stride=BLKIN), :] = piece
        start = min(x * BLK, 2 * BLK * BLK - LANES)
        piece = resample_ref[:, start : start + LANES].astype(f32)
        if start != x * BLK:
            piece = jnp.roll(piece, start - x * BLK, axis=1)
        resample_rows[pl.ds(x, blocks, stride=2 * BLK), :] = piece

    terms = jnp.concatenate(
        [coefficients_ref[:, 4 * NTERMS * r : 4 * NTERMS * (r + 1)] for r in range(4)], axis=0
    )
    spread = jnp.dot(terms, spread_ref[...], preferred_element_type=f32)
    lane = lax.broadcasted_iota(jnp.int32, (blocks, blocks), 1)
    sublane = lax.broadcasted_iota(jnp.int32, (blocks, blocks), 0)
    order = jnp.sum(
        jnp.where(lane == sublane, orders_ref[...].astype(f32), 0.0), axis=1, keepdims=True
    )
    order = jnp.concatenate([order] * 4, axis=0)
    first, second = order >= 1.0, order >= 2.0
    term = [spread[:, wide * m : wide * (m + 1)] for m in range(NTERMS)]
    term = (
        term[:1]
        + [jnp.where(first, t, 0.0) for t in term[1:3]]
        + [jnp.where(second, t, 0.0) for t in term[3:]]
    )
    across = across_ref[0:1, :]
    planes[:, :wide] = term[0] + across * (term[2] + across * term[5])
    planes[:, wide : 2 * wide] = term[1] + across * term[4]
    planes[:, 2 * wide :] = term[3]

    row_id = lax.broadcasted_iota(jnp.int32, (BLK, wide), 0).astype(f32)
    down = (2.0 * row_id + 1.0) / BLK - 1.0

    def step(number, _):
        first_block = number * group
        stacked = jnp.concatenate(
            [
                image_rows[pl.ds(pl.multiple_of((first_block + g) * BLKIN, 8), BLKIN), :]
                for g in range(group)
            ],
            axis=1,
        ).astype(bf16)
        smooth = jnp.dot(row_tables_ref[...], stacked, preferred_element_type=f32).astype(bf16)
        for g in range(group):
            block = first_block + g
            response = jnp.dot(
                smooth[:, LANES * g : LANES * (g + 1)],
                column_tables_ref[...],
                preferred_element_type=f32,
            )
            total = jnp.zeros((BLK, wide), f32)
            for r in range(4):
                plane = planes[pl.ds(r * blocks + block, 1), :]
                weight = plane[:, :wide] + down * (
                    plane[:, wide : 2 * wide] + down * plane[:, 2 * wide :]
                )
                total = total + weight * response[BLK * r : BLK * (r + 1), :]
            low, high = total[:, :LANES], total[:, LANES:]
            folded = (
                low
                + high
                + pltpu.roll(low, LANES - BLK, axis=1)
                + pltpu.roll(low, LANES - 2 * BLK, axis=1)
            )
            matched = folded[:, :BLK].astype(bf16)
            at = pl.multiple_of(block * 2 * BLK, 8)
            left = resample_rows[pl.ds(at, BLK), :][:, :BLK].astype(bf16)
            right = resample_rows[pl.ds(at + BLK, BLK), :][:, :BLK].astype(bf16)
            halfway = jnp.dot(left, matched, preferred_element_type=f32).astype(bf16)
            warped = lax.dot_general(
                halfway, right, (((1,), (1,)), ((), ())), preferred_element_type=f32
            )
            warped_rows[pl.ds(pl.multiple_of(block * BLK, 8), BLK), 0:BLK] = warped
        return 0

    lax.fori_loop(0, blocks // group, step, 0)

    flat[:, 12 * LANES :] = jnp.zeros((blocks, LANES), f32)
    for i in range(BLK):
        flat[:, BLK * i : BLK * (i + 1)] = warped_rows[pl.ds(i, blocks, stride=BLK), 0:BLK]
    pixels = flat[...].astype(bf16)

    slots, pairs = out_ref.shape[0], TOP * blocks
    patch = jnp.concatenate([routes_ref[k : k + 1, :] for k in range(TOP)], axis=1)
    slot = lax.broadcasted_iota(jnp.int32, (slots, pairs), 0)
    hit = jnp.where(patch == slot // 2, 1.0, 0.0)
    before = lax.broadcasted_iota(jnp.int32, (pairs, pairs), 0)
    after = lax.broadcasted_iota(jnp.int32, (pairs, pairs), 1)
    rank = jnp.dot(
        hit.astype(bf16),
        jnp.where(before < after, 1.0, 0.0).astype(bf16),
        preferred_element_type=f32,
    )
    pick = jnp.where(rank == (slot % 2).astype(f32), hit, 0.0).astype(bf16)
    packed = jnp.dot(
        pick, jnp.concatenate([pixels] * TOP, axis=0), preferred_element_type=f32
    )
    column = lax.broadcasted_iota(jnp.int32, (LANES, pairs), 0) - EXTRA
    corner_y = jnp.concatenate([offsets_ref[k, 0:1, :] for k in range(TOP)], axis=1).astype(f32)
    corner_x = jnp.concatenate([offsets_ref[k, 1:2, :] for k in range(TOP)], axis=1).astype(f32)
    weight = jnp.concatenate([weights_ref[...].astype(f32)] * TOP, axis=1)
    extras = jnp.where(
        column == 0,
        corner_y,
        jnp.where(column == 1, corner_x, jnp.where(column == 2, weight, 0.0)),
    ).astype(bf16)
    tail = lax.dot_general(pick, extras, (((1,), (1,)), ((), ())), preferred_element_type=f32)
    out_ref[:, : 12 * LANES] = packed[:, : 12 * LANES].astype(bf16)
    out_ref[:, 12 * LANES :] = (packed[:, 12 * LANES :] + tail).astype(bf16)


def warp_and_pack(images, coefficients, orders, resample, weights, routes, offsets, slots):
    blocks = images.shape[0]
    f32 = jnp.float32
    return pl.pallas_call(
        warp_kernel,
        out_shape=jax.ShapeDtypeStruct((slots, WIDTH), jnp.bfloat16),
        scratch_shapes=[
            pltpu.VMEM((blocks * BLKIN, LANES), f32),
            pltpu.VMEM((blocks * 2 * BLK, LANES), f32),
            pltpu.VMEM((blocks * 4, 3 * 2 * LANES), f32),
            pltpu.VMEM((blocks * BLK, LANES), f32),
            pltpu.VMEM((blocks, WIDTH), f32),
        ],
        compiler_params=pltpu.CompilerParams(vmem_limit_bytes=32 << 20),
        name="warp_and_pack",
    )(
        images,
        coefficients,
        orders,
        resample,
        weights,
        jnp.transpose(routes, (1, 0)),
        jnp.transpose(offsets, (1, 2, 0)),
        *constant_tables(),
    )


def per_device(images, coefficients, orders, resample, weights, routes, offsets):
    visit_count = lax.axis_size("visit")
    tract_count = lax.axis_size("tract")
    capacity = 2
    slot_count = visit_count * capacity
    parcel = warp_and_pack(
        images[0],
        coefficients[0],
        orders,
        resample[0],
        weights,
        routes[0],
        offsets[0],
        slot_count,
    )
    parcel = lax.all_to_all(
        parcel.reshape(visit_count, capacity, WIDTH), "visit", split_axis=0, concat_axis=0, tiled=True
    ).reshape(slot_count, WIDTH)
    warped = parcel[:, : BLK * BLK].reshape(slot_count, BLK, BLK)
    arrived = parcel[:, BLK * BLK : BLK * BLK + 3]
    pixels = jnp.arange(PATCH, dtype=jnp.float32)
    within = jnp.arange(BLK, dtype=jnp.float32)
    row_hit = (
        pixels[None, None, :]
        == arrived[:, 0, None, None].astype(jnp.float32) + within[None, :, None]
    )
    col_hit = (
        pixels[None, None, :]
        == arrived[:, 1, None, None].astype(jnp.float32) + within[None, :, None]
    )
    row_place = jnp.where(row_hit, arrived[:, 2, None, None], jnp.zeros((), jnp.bfloat16))
    col_place = col_hit.astype(jnp.bfloat16)
    spread = jnp.einsum(
        "sij,sjq->siq", warped, col_place, preferred_element_type=jnp.float32
    ).astype(jnp.bfloat16)
    partial = jnp.einsum("sip,siq->pq", row_place, spread, preferred_element_type=jnp.float32)
    row_cover = jnp.sum(row_place.astype(jnp.float32), axis=1).astype(jnp.bfloat16)
    col_cover = jnp.sum(col_place.astype(jnp.float32), axis=1).astype(jnp.bfloat16)
    partial_weight = jnp.einsum(
        "sp,sq->pq", row_cover, col_cover, preferred_element_type=jnp.float32
    )
    rows = PATCH // tract_count
    both = jnp.concatenate(
        [partial.reshape(tract_count, rows, PATCH), partial_weight.reshape(tract_count, rows, PATCH)],
        axis=1,
    ).astype(jnp.bfloat16)
    both = lax.all_to_all(both, "tract", split_axis=0, concat_axis=0, tiled=True)
    sums = jnp.sum(both.astype(jnp.float32), axis=0)
    return (sums[None, :rows], sums[None, rows:])


def solution(mesh):
    in_specs = (
        P("tract", "visit", None),
        P("tract", "visit", None),
        P("tract", "visit"),
        P("tract", "visit", None),
        P("tract", "visit"),
        P("tract", "visit", None),
        P("tract", "visit", None, None),
    )
    out_specs = (P("visit", "tract", None), P("visit", "tract", None))
    return jax.shard_map(
        per_device, mesh=mesh, in_specs=in_specs, out_specs=out_specs, check_vma=False
    )
```

time: 98.3 us -> 90.8 us (0.924)
  matrix products: 23.3 us -> 2.63 us
  Pallas kernels: 0 us -> 15.4 us
  other arithmetic: 6.09 us -> 1.79 us
  local copies, waits for them, and re-layouts: 9.25 us -> 11.3 us
    dot_general x23 -> x0, matrix products: 20.6 us -> none  [the longest x16 15.9 us: match_and_warp(): jnp.einsum('niy,jy->nij', smooth, tables[col_kernel], preferred_element_t...]
    pallas_call x0 -> x1, Pallas kernels: none -> 15.4 us  [warp_and_pack(): pl.pallas_call(warp_kernel, out_shape=jax.ShapeDtypeStruct((slots, WIDTH)...]
    unnamed x5 -> x22, local copies, waits for them, and re-layouts: 1.87 us -> 8.49 us
    another operation x5 -> x0, local copies, waits for them, and re-layouts: 3.27 us -> none  [the longest x1 2.07 us: match_and_warp(): images = flat_images.reshape(-1, BLKIN, BLKIN)]
    reduce_sum x5 -> x0, other arithmetic: 2.73 us -> none  [the longest x4 2.55 us: kernel_tables(): normal_sum = jnp.sum(jnp.abs(profile(tap_offsets)))]
where the time goes in v2:
time: 90.8 us; the launch traced here: 90.2 us
  blocking collectives  58.3 us (64%)
  Pallas kernels  15.4 us (17%)
  local copies, waits for them, and re-layouts  11.3 us (12%)
  matrix products  2.63 us (3%)
  other arithmetic  1.79 us (2%)
    all_to_all x1, blocking collectives, per_device(): lax.all_to_all(parcel.reshape(visit_count, capacity, WIDTH), 'visit', spl...  44.5 us
    pallas_call x1, Pallas kernels, warp_and_pack(): pl.pallas_call(warp_kernel, out_shape=jax.ShapeDtypeStruct((slots, WIDTH)...  15.4 us
    all_to_all x1, blocking collectives, per_device(): lax.all_to_all(both, 'tract', split_axis=0, concat_axis=0, tiled=True)  13.9 us
    unnamed x22, local copies, waits for them, and re-layouts  8.49 us

profile of v2, /device:TPU:1, one launch (start us, length us, event | category | flops | bytes accessed | tf_op | source)
XLA Modules:
  0.0 90.2 jit_solution(4460158823092267494)
XLA Ops:
  0.6 0.0 copy-start
  0.6 1.0 %copy-done = bf16[1,32,6400]{2,1,0:T(8,128)(2,1)S(1)} copy-done((bf16[1,32,6400]{2,1,0:T(8,128)(2,1)S(1)}, bf16[1,32,6400]{2,1,0:T(8,128)(2,1)}, u32[]{:S(2)}) %copy-start) | copy-done | bytes 409624
  1.6 0.0 copy-start.1
  1.6 0.9 %copy-done.1 = bf16[1,32,3200]{2,1,0:T(8,128)(2,1)S(1)} copy-done((bf16[1,32,3200]{2,1,0:T(8,128)(2,1)S(1)}, bf16[1,32,3200]{2,1,0:T(8,128)(2,1)}, u32[]{:S(2)}) %copy-start.1) | copy-done | bytes 204824
  2.6 0.0 copy-start.2
  2.6 0.9 copy-done.2
  3.5 0.0 copy-start.3
  3.5 0.8 copy-done.3
  4.3 0.0 copy-start.4
  4.3 0.8 copy-done.4
  5.1 0.0 copy-start.5
  5.1 0.7 copy-done.5
  5.8 0.0 copy-start.6
  5.8 0.7 copy-done.6
  6.5 0.0 copy-start.7
  6.5 0.7 copy-done.7
  7.1 0.0 copy-start.8
  7.1 0.7 copy-done.8
  7.8 0.0 copy-start.9
  7.8 0.7 copy-done.9
  8.5 0.0 copy-start.10
  8.5 0.7 copy-done.10
  9.1 15.4 %warp_and_pack.1 = bf16[128,1664]{1,0:T(8,128)(2,1)S(1)} custom-call(bf16[32,6400]{1,0:T(8,128)(2,1)S(1)} %bitcast.28, bf16[32,96]{1,0:T(8,128)(2,1)S(1)} %bitcast.30, s32[1,32]{1,0:T(1,128)S(1)} %copy-done.9, bf16[32,3200]{1,0:T(8,128)(2,1)S(1)} %bitcast.29, bf16[1,32]{1,0:T(2,128)(2,1)S(1)} %copy-done.10, s32[2,32]{1,0:T(2,128)S(1)} %bitcast.32, ...), custom_call_target="tpu_custom_call" | custom-call | tf_op jit(solution)/shard_map/warp_and_pack/pallas_call | solution.py:204
  24.6 0.2 reshape.86
  24.7 44.5 %all_to_all.10 = bf16[64,2,1664]{2,1,0:T(2,128)(2,1)S(1)} all-to-all(bf16[64,2,1664]{2,1,0:T(2,128)(2,1)S(1)} %reshape.86), channel_id=1, replica_groups=mesh['tract'=8,'visit'=64] {'visit'}, dimensions={0} | all-to-all | bytes 851968 | tf_op jit(solution)/shard_map/all_to_all | solution.py:243
  69.2 0.2 reshape.87
  69.4 0.2 slice_reduce_fusion
  69.6 0.2 convert_reduce_fusion.1
  69.8 0.1 iota_add_fusion
  69.9 0.9 fusion.6
  70.8 0.2 copy.14
  71.0 1.5 %copy.15 = bf16[128,40,40]{2,1,0:T(8,128)(2,1)S(1)} copy(bf16[128,40,40]{0,2,1:T(8,128)(2,1)S(1)} %bitcast.34) | data formatting | bytes 819200 | tf_op jit(solution)/shard_map/reshape | solution.py:246
  72.5 1.6 %fusion.10 = bf16[128,40,256]{2,1,0:T(8,128)(2,1)S(1)} fusion(bf16[128,40,40]{2,1,0:T(8,128)(2,1)S(1)} %copy.15, f32[128,40]{1,0:T(8,128)S(1)} %iota_add_fusion), kind=kOutput, calls=%fused_computation.11 | convolution fusion | flops 107479040 | bytes 3051520 | tf_op jit(solution)/shard_map/sij,sjq->siq/dot_general | solution.py:260
  74.0 0.6 fusion.3
  74.6 0.9 fusion.18
  75.5 0.2 convolution_convert_fusion
  75.7 13.9 %all_to_all.11 = bf16[8,64,256]{2,1,0:T(8,128)(2,1)S(1)} all-to-all(bf16[8,64,256]{2,1,0:T(8,128)(2,1)S(1)} %pad_maximum_fusion), channel_id=1, replica_groups=mesh['tract'=8,'visit'=64] {'tract'}, dimensions={0} | all-to-all | bytes 524288 | tf_op jit(solution)/shard_map/all_to_all | solution.py:274
  89.6 0.6 slice_bitcast_fusion
  (3 shorter events, 0.1 us)
Async XLA Ops:
  0.6 1.0 %copy-start = (bf16[1,32,6400]{2,1,0:T(8,128)(2,1)S(1)}, bf16[1,32,6400]{2,1,0:T(8,128)(2,1)}, u32[]{:S(2)}) copy-start(bf16[1,32,6400]{2,1,0:T(8,128)(2,1)} %param.11) | copy-start | bytes 1228804
  1.6 0.9 %copy-start.1 = (bf16[1,32,3200]{2,1,0:T(8,128)(2,1)S(1)}, bf16[1,32,3200]{2,1,0:T(8,128)(2,1)}, u32[]{:S(2)}) copy-start(bf16[1,32,3200]{2,1,0:T(8,128)(2,1)} %param.14) | copy-start | bytes 614404
  2.6 0.9 copy-start.2
  3.5 0.8 copy-start.3
  4.3 0.8 copy-start.4
  5.1 0.7 copy-start.5
  5.8 0.7 copy-start.6
  6.5 0.7 copy-start.7
  7.1 0.7 copy-start.8
  7.8 0.7 copy-start.9
  8.5 0.7 copy-start.10

commit v3 on v2

--- a/solution.py
+++ b/solution.py
@@ -77,10 +77,46 @@
     planes,
     warped_rows,
     flat,
+    *held,
 ):
     f32, bf16 = jnp.float32, jnp.bfloat16
+    *held, arrival = held
+    sources = (
+        images_ref,
+        resample_ref,
+        coefficients_ref,
+        orders_ref,
+        weights_ref,
+        routes_ref,
+        offsets_ref,
+        row_tables_ref,
+        column_tables_ref,
+        spread_ref,
+        across_ref,
+    )
+    copies = [
+        pltpu.make_async_copy(source, kept, arrival.at[number])
+        for number, (source, kept) in enumerate(zip(sources, held, strict=True))
+    ]
+    for copy in copies:
+        copy.start()
+    (
+        images_ref,
+        resample_ref,
+        coefficients_ref,
+        orders_ref,
+        weights_ref,
+        routes_ref,
+        offsets_ref,
+        row_tables_ref,
+        column_tables_ref,
+        spread_ref,
+        across_ref,
+    ) = held
+    for copy in copies[2:]:
+        copy.wait()
+    copies[0].wait()
     blocks = images_ref.shape[0]
-    group = 4
     wide = 2 * LANES
 
     for x in range(BLKIN):
@@ -88,12 +124,14 @@
         piece = images_ref[:, start : start + LANES].astype(f32)
         if start != x * BLKIN:
             piece = jnp.roll(piece, start - x * BLKIN, axis=1)
-        image_rows[pl.ds(x, blocks, stride=BLKIN), :] = piece
+        image_rows[pl.ds(x, blocks, stride=BLKIN + 1), :] = piece
+    copies[1].wait()
+    for x in range(2 * BLK):
         start = min(x * BLK, 2 * BLK * BLK - LANES)
         piece = resample_ref[:, start : start + LANES].astype(f32)
         if start != x * BLK:
             piece = jnp.roll(piece, start - x * BLK, axis=1)
-        resample_rows[pl.ds(x, blocks, stride=2 * BLK), :] = piece
+        resample_rows[pl.ds(x, blocks, stride=2 * BLK + 1), :] = piece
 
     terms = jnp.concatenate(
         [coefficients_ref[:, 4 * NTERMS * r : 4 * NTERMS * (r + 1)] for r in range(4)], axis=0
@@ -120,53 +158,61 @@
     row_id = lax.broadcasted_iota(jnp.int32, (BLK, wide), 0).astype(f32)
     down = (2.0 * row_id + 1.0) / BLK - 1.0
 
-    def step(number, _):
-        first_block = number * group
-        stacked = jnp.concatenate(
-            [
-                image_rows[pl.ds(pl.multiple_of((first_block + g) * BLKIN, 8), BLKIN), :]
-                for g in range(group)
-            ],
-            axis=1,
+    stacked = jnp.concatenate(
+        [
+            image_rows[(BLKIN + 1) * g : (BLKIN + 1) * g + BLKIN, :]
+            for g in range(blocks)
+        ],
+        axis=1,
+    ).astype(bf16)
+    smooth = jnp.dot(row_tables_ref[...], stacked, preferred_element_type=f32).astype(bf16)
+    responses = [
+        jnp.dot(
+            smooth[:, LANES * g : LANES * (g + 1)],
+            column_tables_ref[...],
+            preferred_element_type=f32,
+        )
+        for g in range(blocks)
+    ]
+    matched = []
+    for g in range(blocks):
+        total = jnp.zeros((BLK, wide), f32)
+        for r in range(4):
+            plane = planes[r * blocks + g : r * blocks + g + 1, :]
+            weight = plane[:, :wide] + down * (
+                plane[:, wide : 2 * wide] + down * plane[:, 2 * wide :]
+            )
+            total = total + weight * responses[g][BLK * r : BLK * (r + 1), :]
+        low, high = total[:, :LANES], total[:, LANES:]
+        folded = (
+            low
+            + high
+            + pltpu.roll(low, LANES - BLK, axis=1)
+            + pltpu.roll(low, LANES - 2 * BLK, axis=1)
+        )
+        matched.append(folded[:, :BLK].astype(bf16))
+    halfway = [
+        jnp.dot(
+            resample_rows[(2 * BLK + 1) * g : (2 * BLK + 1) * g + BLK, :][:, :BLK].astype(bf16),
+            matched[g],
+            preferred_element_type=f32,
         ).astype(bf16)
-        smooth = jnp.dot(row_tables_ref[...], stacked, preferred_element_type=f32).astype(bf16)
-        for g in range(group):
-            block = first_block + g
-            response = jnp.dot(
-                smooth[:, LANES * g : LANES * (g + 1)],
-                column_tables_ref[...],
-                preferred_element_type=f32,
-            )
-            total = jnp.zeros((BLK, wide), f32)
-            for r in range(4):
-                plane = planes[pl.ds(r * blocks + block, 1), :]
-                weight = plane[:, :wide] + down * (
-                    plane[:, wide : 2 * wide] + down * plane[:, 2 * wide :]
-                )
-                total = total + weight * response[BLK * r : BLK * (r + 1), :]
-            low, high = total[:, :LANES], total[:, LANES:]
-            folded = (
-                low
-                + high
-                + pltpu.roll(low, LANES - BLK, axis=1)
-                + pltpu.roll(low, LANES - 2 * BLK, axis=1)
-            )
-            matched = folded[:, :BLK].astype(bf16)
-            at = pl.multiple_of(block * 2 * BLK, 8)
-            left = resample_rows[pl.ds(at, BLK), :][:, :BLK].astype(bf16)
-            right = resample_rows[pl.ds(at + BLK, BLK), :][:, :BLK].astype(bf16)
-            halfway = jnp.dot(left, matched, preferred_element_type=f32).astype(bf16)
-            warped = lax.dot_general(
-                halfway, right, (((1,), (1,)), ((), ())), preferred_element_type=f32
-            )
-            warped_rows[pl.ds(pl.multiple_of(block * BLK, 8), BLK), 0:BLK] = warped
-        return 0
-
-    lax.fori_loop(0, blocks // group, step, 0)
-
+        for g in range(blocks)
+    ]
+    warped = [
+        lax.dot_general(
+            halfway[g],
+            resample_rows[(2 * BLK + 1) * g + BLK : (2 * BLK + 1) * (g + 1) - 1, :][:, :BLK].astype(bf16),
+            (((1,), (1,)), ((), ())),
+            preferred_element_type=f32,
+        )
+        for g in range(blocks)
+    ]
+    for g in range(blocks):
+        warped_rows[(BLK + 1) * g : (BLK + 1) * g + BLK, 0:BLK] = warped[g]
     flat[:, 12 * LANES :] = jnp.zeros((blocks, LANES), f32)
     for i in range(BLK):
-        flat[:, BLK * i : BLK * (i + 1)] = warped_rows[pl.ds(i, blocks, stride=BLK), 0:BLK]
+        flat[:, BLK * i : BLK * (i + 1)] = warped_rows[pl.ds(i, blocks, stride=BLK + 1), 0:BLK]
     pixels = flat[...].astype(bf16)
 
     slots, pairs = out_ref.shape[0], TOP * blocks
@@ -201,19 +247,7 @@
 def warp_and_pack(images, coefficients, orders, resample, weights, routes, offsets, slots):
     blocks = images.shape[0]
     f32 = jnp.float32
-    return pl.pallas_call(
-        warp_kernel,
-        out_shape=jax.ShapeDtypeStruct((slots, WIDTH), jnp.bfloat16),
-        scratch_shapes=[
-            pltpu.VMEM((blocks * BLKIN, LANES), f32),
-            pltpu.VMEM((blocks * 2 * BLK, LANES), f32),
-            pltpu.VMEM((blocks * 4, 3 * 2 * LANES), f32),
-            pltpu.VMEM((blocks * BLK, LANES), f32),
-            pltpu.VMEM((blocks, WIDTH), f32),
-        ],
-        compiler_params=pltpu.CompilerParams(vmem_limit_bytes=32 << 20),
-        name="warp_and_pack",
-    )(
+    operands = (
         images,
         coefficients,
         orders,
@@ -223,6 +257,100 @@
         jnp.transpose(offsets, (1, 2, 0)),
         *constant_tables(),
     )
+    kept = [operands[n] for n in (0, 3, 1, 2, 4, 5, 6, 7, 8, 9, 10)]
+    return pl.pallas_call(
+        warp_kernel,
+        out_shape=jax.ShapeDtypeStruct((slots, WIDTH), jnp.bfloat16),
+        in_specs=[pl.BlockSpec(memory_space=pl.ANY)] * len(operands),
+        scratch_shapes=[
+            pltpu.VMEM((blocks * (BLKIN + 1), LANES), f32),
+            pltpu.VMEM((blocks * (2 * BLK + 1), LANES), f32),
+            pltpu.VMEM((blocks * 4, 3 * 2 * LANES), f32),
+            pltpu.VMEM((blocks * (BLK + 1), LANES), f32),
+            pltpu.VMEM((blocks, WIDTH), f32),
+            *[pltpu.VMEM(array.shape, array.dtype) for array in kept],
+            pltpu.SemaphoreType.DMA((len(kept),)),
+        ],
+        compiler_params=pltpu.CompilerParams(vmem_limit_bytes=56 << 20),
+        name="warp_and_pack",
+    )(*operands)
+
+
+def place_kernel(parcel_ref, out_ref, slot_rows, spread_left, spread_right, corner_x_wide):
+    f32, bf16 = jnp.float32, jnp.bfloat16
+    slots = parcel_ref.shape[0]
+    tracts, rows = out_ref.shape[0], PATCH // out_ref.shape[0]
+    pitch = slots + 1
+
+    for i in range(BLK):
+        start = min(i * BLK, WIDTH - LANES)
+        piece = parcel_ref[:, start : start + LANES].astype(f32)
+        if start != i * BLK:
+            piece = jnp.roll(piece, start - i * BLK, axis=1)
+        slot_rows[pl.ds(i, slots, stride=BLK + 1), :] = piece
+    tail = parcel_ref[:, WIDTH - LANES :].astype(f32)
+    corner_x = tail[:, EXTRA + 1 : EXTRA + 2]
+    corner_x_wide[...] = jnp.broadcast_to(corner_x, (slots, PATCH))
+    by_slot = jnp.transpose(tail, (1, 0))
+    corner_y = by_slot[EXTRA : EXTRA + 1, :]
+    weight = by_slot[EXTRA + 2 : EXTRA + 3, :]
+
+    shift = (
+        lax.broadcasted_iota(jnp.int32, (BLK, PATCH), 1)
+        - lax.broadcasted_iota(jnp.int32, (BLK, PATCH), 0)
+    ).astype(f32)
+    batch = 16
+    for first in range(0, slots, batch):
+        placed = []
+        for s in range(first, first + batch):
+            column = jnp.where(shift == corner_x_wide[s : s + 1, :], 1.0, 0.0).astype(bf16)
+            block = slot_rows[(BLK + 1) * s : (BLK + 1) * s + BLK, :][:, :BLK].astype(bf16)
+            placed.append(jnp.dot(block, column, preferred_element_type=f32))
+        for s in range(first, first + batch):
+            spread_left[pl.ds(s, BLK, stride=pitch), :] = placed[s - first][:, :LANES]
+            spread_right[pl.ds(s, BLK, stride=pitch), :] = placed[s - first][:, LANES:]
+
+    above = lax.broadcasted_iota(jnp.int32, (PATCH, slots), 0).astype(f32) - corner_y
+    flux = jnp.zeros((PATCH, PATCH), f32)
+    depth = 2
+    for i in range(0, BLK, depth):
+        row = jnp.concatenate(
+            [jnp.where(above == float(i + n), weight, 0.0).astype(bf16) for n in range(depth)], axis=1
+        )
+        across = jnp.concatenate(
+            [
+                jnp.concatenate(
+                    [half[pitch * (i + n) : pitch * (i + n) + slots, :] for n in range(depth)], axis=0
+                )
+                for half in (spread_left, spread_right)
+            ],
+            axis=1,
+        ).astype(bf16)
+        flux += jnp.dot(row, across, preferred_element_type=f32)
+    beside = lax.broadcasted_iota(jnp.int32, (slots, PATCH), 1).astype(f32) - corner_x
+    row_cover = jnp.where((above >= 0.0) & (above < float(BLK)), weight, 0.0).astype(bf16)
+    column_cover = jnp.where((beside >= 0.0) & (beside < float(BLK)), 1.0, 0.0).astype(bf16)
+    cover = jnp.dot(row_cover, column_cover, preferred_element_type=f32)
+    for t in range(tracts):
+        out_ref[t, :rows, :] = flux[rows * t : rows * (t + 1), :].astype(bf16)
+        out_ref[t, rows:, :] = cover[rows * t : rows * (t + 1), :].astype(bf16)
+
+
+def place(parcel, tracts):
+    slots = parcel.shape[0]
+    f32 = jnp.float32
+    return pl.pallas_call(
+        place_kernel,
+        out_shape=jax.ShapeDtypeStruct((tracts, 2 * PATCH // tracts, PATCH), jnp.bfloat16),
+        scratch_shapes=[
+            pltpu.VMEM((slots * (BLK + 1), LANES), f32),
+            pltpu.VMEM(((slots + 1) * BLK, LANES), f32),
+            pltpu.VMEM(((slots + 1) * BLK, LANES), f32),
+            pltpu.VMEM((slots, PATCH), f32),
+        ],
+        compiler_params=pltpu.CompilerParams(vmem_limit_bytes=24 << 20),
+        name="place_in_patch",
+    )(parcel)
 
 
 def per_device(images, coefficients, orders, resample, weights, routes, offsets):
@@ -243,36 +371,10 @@
     parcel = lax.all_to_all(
         parcel.reshape(visit_count, capacity, WIDTH), "visit", split_axis=0, concat_axis=0, tiled=True
     ).reshape(slot_count, WIDTH)
-    warped = parcel[:, : BLK * BLK].reshape(slot_count, BLK, BLK)
-    arrived = parcel[:, BLK * BLK : BLK * BLK + 3]
-    pixels = jnp.arange(PATCH, dtype=jnp.float32)
-    within = jnp.arange(BLK, dtype=jnp.float32)
-    row_hit = (
-        pixels[None, None, :]
-        == arrived[:, 0, None, None].astype(jnp.float32) + within[None, :, None]
-    )
-    col_hit = (
-        pixels[None, None, :]
-        == arrived[:, 1, None, None].astype(jnp.float32) + within[None, :, None]
-    )
-    row_place = jnp.where(row_hit, arrived[:, 2, None, None], jnp.zeros((), jnp.bfloat16))
-    col_place = col_hit.astype(jnp.bfloat16)
-    spread = jnp.einsum(
-        "sij,sjq->siq", warped, col_place, preferred_element_type=jnp.float32
-    ).astype(jnp.bfloat16)
-    partial = jnp.einsum("sip,siq->pq", row_place, spread, preferred_element_type=jnp.float32)
-    row_cover = jnp.sum(row_place.astype(jnp.float32), axis=1).astype(jnp.bfloat16)
-    col_cover = jnp.sum(col_place.astype(jnp.float32), axis=1).astype(jnp.bfloat16)
-    partial_weight = jnp.einsum(
-        "sp,sq->pq", row_cover, col_cover, preferred_element_type=jnp.float32
-    )
-    rows = PATCH // tract_count
-    both = jnp.concatenate(
-        [partial.reshape(tract_count, rows, PATCH), partial_weight.reshape(tract_count, rows, PATCH)],
-        axis=1,
-    ).astype(jnp.bfloat16)
+    both = place(parcel, tract_count)
     both = lax.all_to_all(both, "tract", split_axis=0, concat_axis=0, tiled=True)
     sums = jnp.sum(both.astype(jnp.float32), axis=0)
+    rows = PATCH // tract_count
     return (sums[None, :rows], sums[None, rows:])
 
 

time: 90.8 us -> 68.3 us (0.75)
  local copies, waits for them, and re-layouts: 11.3 us -> 1.96 us
  Pallas kernels: 15.4 us -> 7.09 us
  matrix products: 2.63 us -> 0 us
  other arithmetic: 1.79 us -> 0.04 us
    pallas_call x1, Pallas kernels: 15.4 us -> 5.1 us  [warp_and_pack(): pl.pallas_call(warp_kernel, out_shape=jax.ShapeDtypeStruct((slots, WIDTH)...]
    unnamed x22 -> x0, local copies, waits for them, and re-layouts: 8.49 us -> none
    dot_general x3 -> x0, matrix products: 2.63 us -> none  [the longest x1 1.57 us: per_device(): jnp.einsum('sij,sjq->siq', warped, col_place, preferred_element_type=jnp....]
    pallas_call x0 -> x1, Pallas kernels: none -> 1.99 us  [place(): pl.pallas_call(place_kernel, out_shape=jax.ShapeDtypeStruct((tracts, 2 *...]
    reshape x1 -> x0, local copies, waits for them, and re-layouts: 1.46 us -> none  [per_device(): warped = parcel[:, :BLK * BLK].reshape(slot_count, BLK, BLK)]
    reduce_sum x2 -> x0, other arithmetic: 1.45 us -> none  [the longest x1 0.89 us: per_device(): jnp.sum(col_place.astype(jnp.float32), axis=1).astype(jnp.bfloat16)]
    reshape x1, local copies, waits for them, and re-layouts: 0.16 us -> 1.17 us  [per_device(): parcel.reshape(visit_count, capacity, WIDTH)]
where the time goes in v3:
time: 68.3 us; the launch traced here: 68.1 us
  blocking collectives  58.3 us (85%)
  Pallas kernels  7.09 us (10%)
  local copies, waits for them, and re-layouts  1.96 us (3%)
    all_to_all x1, blocking collectives, per_device(): lax.all_to_all(parcel.reshape(visit_count, capacity, WIDTH), 'visit', spl...  44.5 us
    all_to_all x1, blocking collectives, per_device(): lax.all_to_all(both, 'tract', split_axis=0, concat_axis=0, tiled=True)  13.9 us
    pallas_call x1, Pallas kernels, warp_and_pack(): pl.pallas_call(warp_kernel, out_shape=jax.ShapeDtypeStruct((slots, WIDTH)...  5.1 us
    pallas_call x1, Pallas kernels, place(): pl.pallas_call(place_kernel, out_shape=jax.ShapeDtypeStruct((tracts, 2 *...  1.99 us

profile of v3, /device:TPU:1, one launch (start us, length us, event | category | flops | bytes accessed | tf_op | source)
XLA Modules:
  0.0 68.1 jit_solution(882922387939299651)
XLA Ops:
  0.6 5.1 %warp_and_pack.1 = bf16[128,1664]{1,0:T(8,128)(2,1)} custom-call(bf16[32,6400]{1,0:T(8,128)(2,1)} %bitcast.13, bf16[32,96]{1,0:T(8,128)(2,1)} %bitcast.15, s32[1,32]{1,0:T(1,128)} %orders_ref.1, bf16[32,3200]{1,0:T(8,128)(2,1)} %bitcast.14, bf16[1,32]{1,0:T(2,128)(2,1)} %weights_ref.1, s32[2,32]{1,0:T(2,128)} %bitcast.17, s32[2,2,32]{2,1,0:T(2,128)} %bitcast.16, ...), custom_call_target="tpu_custom_call" | custom-call | tf_op jit(solution)/shard_map/warp_and_pack/pallas_call | solution.py:261
  5.7 1.2 %reshape.10 = bf16[64,2,1664]{2,1,0:T(2,128)(2,1)S(1)} reshape(bf16[128,1664]{1,0:T(8,128)(2,1)} %warp_and_pack.1) | data formatting | bytes 851968 | tf_op jit(solution)/shard_map/reshape | solution.py:372
  6.9 44.5 %all_to_all.10 = bf16[64,2,1664]{2,1,0:T(2,128)(2,1)S(1)} all-to-all(bf16[64,2,1664]{2,1,0:T(2,128)(2,1)S(1)} %reshape.10), channel_id=1, replica_groups=mesh['tract'=8,'visit'=64] {'visit'}, dimensions={0} | all-to-all | bytes 851968 | tf_op jit(solution)/shard_map/all_to_all | solution.py:371
  51.4 0.2 reshape.11.parcel_ref
  51.5 2.0 %place_in_patch.1 = bf16[8,64,256]{2,1,0:T(8,128)(2,1)S(1)} custom-call(bf16[128,1664]{1,0:T(8,128)(2,1)S(1)} %reshape.11.parcel_ref), custom_call_target="tpu_custom_call" | custom-call | tf_op jit(solution)/shard_map/place_in_patch/pallas_call | solution.py:342
  53.5 13.9 %all_to_all.11 = bf16[8,64,256]{2,1,0:T(8,128)(2,1)S(1)} all-to-all(bf16[8,64,256]{2,1,0:T(8,128)(2,1)S(1)} %place_in_patch.1), channel_id=1, replica_groups=mesh['tract'=8,'visit'=64] {'tract'}, dimensions={0} | all-to-all | bytes 524288 | tf_op jit(solution)/shard_map/all_to_all | solution.py:375
  67.4 0.6 slice_bitcast_fusion
  (1 shorter events, 0.0 us)

commit v4 on v3

--- a/solution.py
+++ b/solution.py
@@ -41,22 +41,11 @@
 
         total = np.sum(np.abs(profile(taps)), dtype=np.float32)
         tables.append(np.where(inside, profile(shifted) / total, np.float32(0.0)))
-    centres = ((2.0 * np.arange(BLK, dtype=np.float32) + 1.0) / BLK - 1.0).astype(np.float32)
-    row_tables = np.concatenate(tables, axis=0)
-    column_tables = np.zeros((LANES, 2 * LANES), np.float32)
-    spread = np.zeros((4 * NTERMS, NTERMS, 2 * LANES), np.float32)
-    across = np.zeros((8, 2 * LANES), np.float32)
+    held = np.zeros((4 * BLK + LANES, 2 * LANES), np.float32)
+    held[: 4 * BLK, :BLKIN] = np.concatenate(tables, axis=0)
     for c, at in enumerate(COLUMN_AT):
-        column_tables[:BLKIN, at : at + BLK] = tables[c].T
-        across[:, at : at + BLK] = centres
-        for m in range(NTERMS):
-            spread[c * NTERMS + m, m, at : at + BLK] = 1.0
-    return (
-        jnp.asarray(row_tables, jnp.bfloat16),
-        jnp.asarray(column_tables, jnp.bfloat16),
-        jnp.asarray(spread.reshape(4 * NTERMS, NTERMS * 2 * LANES), jnp.bfloat16),
-        jnp.asarray(across),
-    )
+        held[4 * BLK : 4 * BLK + BLKIN, at : at + BLK] = tables[c].T
+    return jnp.asarray(held, jnp.bfloat16)
 
 
 def warp_kernel(
@@ -67,10 +56,7 @@
     weights_ref,
     routes_ref,
     offsets_ref,
-    row_tables_ref,
-    column_tables_ref,
-    spread_ref,
-    across_ref,
+    tables_ref,
     out_ref,
     image_rows,
     resample_rows,
@@ -89,10 +75,7 @@
         weights_ref,
         routes_ref,
         offsets_ref,
-        row_tables_ref,
-        column_tables_ref,
-        spread_ref,
-        across_ref,
+        tables_ref,
     )
     copies = [
         pltpu.make_async_copy(source, kept, arrival.at[number])
@@ -108,13 +91,8 @@
         weights_ref,
         routes_ref,
         offsets_ref,
-        row_tables_ref,
-        column_tables_ref,
-        spread_ref,
-        across_ref,
+        tables_ref,
     ) = held
-    for copy in copies[2:]:
-        copy.wait()
     copies[0].wait()
     blocks = images_ref.shape[0]
     wide = 2 * LANES
@@ -126,6 +104,8 @@
             piece = jnp.roll(piece, start - x * BLKIN, axis=1)
         image_rows[pl.ds(x, blocks, stride=BLKIN + 1), :] = piece
     copies[1].wait()
+    for copy in copies[2:]:
+        copy.wait()
     for x in range(2 * BLK):
         start = min(x * BLK, 2 * BLK * BLK - LANES)
         piece = resample_ref[:, start : start + LANES].astype(f32)
@@ -136,7 +116,17 @@
     terms = jnp.concatenate(
         [coefficients_ref[:, 4 * NTERMS * r : 4 * NTERMS * (r + 1)] for r in range(4)], axis=0
     )
-    spread = jnp.dot(terms, spread_ref[...], preferred_element_type=f32)
+    term_id = lax.broadcasted_iota(jnp.int32, (4 * NTERMS, wide), 0)
+    lane = lax.broadcasted_iota(jnp.int32, (4 * NTERMS, wide), 1)
+    column_kernel = sum((lane >= at).astype(jnp.int32) for at in COLUMN_AT[1:])
+    spread = jnp.concatenate(
+        [
+            jnp.where(term_id == NTERMS * column_kernel + m, 1.0, 0.0).astype(bf16)
+            for m in range(NTERMS)
+        ],
+        axis=1,
+    )
+    spread = jnp.dot(terms, spread, preferred_element_type=f32)
     lane = lax.broadcasted_iota(jnp.int32, (blocks, blocks), 1)
     sublane = lax.broadcasted_iota(jnp.int32, (blocks, blocks), 0)
     order = jnp.sum(
@@ -150,7 +140,11 @@
         + [jnp.where(first, t, 0.0) for t in term[1:3]]
         + [jnp.where(second, t, 0.0) for t in term[3:]]
     )
-    across = across_ref[0:1, :]
+    lane = lax.broadcasted_iota(jnp.int32, (1, wide), 1)
+    within = lane
+    for at in COLUMN_AT[1:]:
+        within = jnp.where(lane >= at, lane - at, within)
+    across = (2.0 * within.astype(f32) + 1.0) / BLK - 1.0
     planes[:, :wide] = term[0] + across * (term[2] + across * term[5])
     planes[:, wide : 2 * wide] = term[1] + across * term[4]
     planes[:, 2 * wide :] = term[3]
@@ -165,11 +159,11 @@
         ],
         axis=1,
     ).astype(bf16)
-    smooth = jnp.dot(row_tables_ref[...], stacked, preferred_element_type=f32).astype(bf16)
+    smooth = jnp.dot(tables_ref[: 4 * BLK, :BLKIN], stacked, preferred_element_type=f32).astype(bf16)
     responses = [
         jnp.dot(
             smooth[:, LANES * g : LANES * (g + 1)],
-            column_tables_ref[...],
+            tables_ref[4 * BLK :, :],
             preferred_element_type=f32,
         )
         for g in range(blocks)
@@ -215,7 +209,7 @@
         flat[:, BLK * i : BLK * (i + 1)] = warped_rows[pl.ds(i, blocks, stride=BLK + 1), 0:BLK]
     pixels = flat[...].astype(bf16)
 
-    slots, pairs = out_ref.shape[0], TOP * blocks
+    slots, pairs = out_ref.shape[0] * out_ref.shape[1], TOP * blocks
     patch = jnp.concatenate([routes_ref[k : k + 1, :] for k in range(TOP)], axis=1)
     slot = lax.broadcasted_iota(jnp.int32, (slots, pairs), 0)
     hit = jnp.where(patch == slot // 2, 1.0, 0.0)
@@ -240,8 +234,8 @@
         jnp.where(column == 1, corner_x, jnp.where(column == 2, weight, 0.0)),
     ).astype(bf16)
     tail = lax.dot_general(pick, extras, (((1,), (1,)), ((), ())), preferred_element_type=f32)
-    out_ref[:, : 12 * LANES] = packed[:, : 12 * LANES].astype(bf16)
-    out_ref[:, 12 * LANES :] = (packed[:, 12 * LANES :] + tail).astype(bf16)
+    packed = jnp.concatenate([packed[:, : 12 * LANES], packed[:, 12 * LANES :] + tail], axis=1)
+    out_ref[...] = packed.astype(bf16).reshape(out_ref.shape)
 
 
 def warp_and_pack(images, coefficients, orders, resample, weights, routes, offsets, slots):
@@ -255,12 +249,12 @@
         weights,
         jnp.transpose(routes, (1, 0)),
         jnp.transpose(offsets, (1, 2, 0)),
-        *constant_tables(),
-    )
-    kept = [operands[n] for n in (0, 3, 1, 2, 4, 5, 6, 7, 8, 9, 10)]
+        constant_tables(),
+    )
+    kept = [operands[n] for n in (0, 3, 1, 2, 4, 5, 6, 7)]
     return pl.pallas_call(
         warp_kernel,
-        out_shape=jax.ShapeDtypeStruct((slots, WIDTH), jnp.bfloat16),
+        out_shape=jax.ShapeDtypeStruct((slots // 2, 2, WIDTH), jnp.bfloat16),
         in_specs=[pl.BlockSpec(memory_space=pl.ANY)] * len(operands),
         scratch_shapes=[
             pltpu.VMEM((blocks * (BLKIN + 1), LANES), f32),
@@ -293,6 +287,7 @@
     corner_x_wide[...] = jnp.broadcast_to(corner_x, (slots, PATCH))
     by_slot = jnp.transpose(tail, (1, 0))
     corner_y = by_slot[EXTRA : EXTRA + 1, :]
+    corner_x_row = by_slot[EXTRA + 1 : EXTRA + 2, :]
     weight = by_slot[EXTRA + 2 : EXTRA + 3, :]
 
     shift = (
@@ -327,13 +322,12 @@
             axis=1,
         ).astype(bf16)
         flux += jnp.dot(row, across, preferred_element_type=f32)
-    beside = lax.broadcasted_iota(jnp.int32, (slots, PATCH), 1).astype(f32) - corner_x
-    row_cover = jnp.where((above >= 0.0) & (above < float(BLK)), weight, 0.0).astype(bf16)
-    column_cover = jnp.where((beside >= 0.0) & (beside < float(BLK)), 1.0, 0.0).astype(bf16)
-    cover = jnp.dot(row_cover, column_cover, preferred_element_type=f32)
+    blank = jnp.zeros((6, PATCH), f32)
     for t in range(tracts):
-        out_ref[t, :rows, :] = flux[rows * t : rows * (t + 1), :].astype(bf16)
-        out_ref[t, rows:, :] = cover[rows * t : rows * (t + 1), :].astype(bf16)
+        corners = jnp.concatenate([corner_y - float(rows * t), corner_x_row], axis=1)
+        weights = jnp.concatenate([weight, jnp.zeros_like(weight)], axis=1)
+        parts = [flux[rows * t : rows * (t + 1), :], corners, weights, blank]
+        out_ref[t] = jnp.concatenate(parts, axis=0).astype(bf16)
 
 
 def place(parcel, tracts):
@@ -341,7 +335,7 @@
     f32 = jnp.float32
     return pl.pallas_call(
         place_kernel,
-        out_shape=jax.ShapeDtypeStruct((tracts, 2 * PATCH // tracts, PATCH), jnp.bfloat16),
+        out_shape=jax.ShapeDtypeStruct((tracts, PATCH // tracts + 8, PATCH), jnp.bfloat16),
         scratch_shapes=[
             pltpu.VMEM((slots * (BLK + 1), LANES), f32),
             pltpu.VMEM(((slots + 1) * BLK, LANES), f32),
@@ -351,6 +345,41 @@
         compiler_params=pltpu.CompilerParams(vmem_limit_bytes=24 << 20),
         name="place_in_patch",
     )(parcel)
+
+
+def finish_kernel(parts_ref, flux_ref, cover_ref):
+    f32, bf16 = jnp.float32, jnp.bfloat16
+    rows, slots = flux_ref.shape[0], PATCH // 2
+    y = lax.broadcasted_iota(jnp.int32, (rows, slots), 0).astype(f32)
+    x = lax.broadcasted_iota(jnp.int32, (PATCH, slots), 0).astype(f32)
+    flux = jnp.zeros((rows, PATCH), f32)
+    cover = jnp.zeros((rows, PATCH), f32)
+    for t in range(parts_ref.shape[0]):
+        part = parts_ref[t].astype(f32)
+        flux += part[:rows, :]
+        extras = part[rows:, :]
+        down = y - extras[0:1, :slots]
+        across = x - extras[0:1, slots:]
+        row = jnp.where((down >= 0.0) & (down < float(BLK)), extras[1:2, :slots], 0.0)
+        column = jnp.where((across >= 0.0) & (across < float(BLK)), 1.0, 0.0)
+        cover += lax.dot_general(
+            row.astype(bf16),
+            column.astype(bf16),
+            (((1,), (1,)), ((), ())),
+            preferred_element_type=f32,
+        )
+    flux_ref[...] = flux
+    cover_ref[...] = cover
+
+
+def finish(parts, tracts):
+    out = jax.ShapeDtypeStruct((PATCH // tracts, PATCH), jnp.float32)
+    return pl.pallas_call(
+        finish_kernel,
+        out_shape=(out, out),
+        compiler_params=pltpu.CompilerParams(vmem_limit_bytes=16 << 20),
+        name="finish",
+    )(parts)
 
 
 def per_device(images, coefficients, orders, resample, weights, routes, offsets):
@@ -369,13 +398,12 @@
         slot_count,
     )
     parcel = lax.all_to_all(
-        parcel.reshape(visit_count, capacity, WIDTH), "visit", split_axis=0, concat_axis=0, tiled=True
+        parcel, "visit", split_axis=0, concat_axis=0, tiled=True
     ).reshape(slot_count, WIDTH)
-    both = place(parcel, tract_count)
-    both = lax.all_to_all(both, "tract", split_axis=0, concat_axis=0, tiled=True)
-    sums = jnp.sum(both.astype(jnp.float32), axis=0)
-    rows = PATCH // tract_count
-    return (sums[None, :rows], sums[None, rows:])
+    parts = place(parcel, tract_count)
+    parts = lax.all_to_all(parts, "tract", split_axis=0, concat_axis=0, tiled=True)
+    flux, cover = finish(parts, tract_count)
+    return (flux[None], cover[None])
 
 
 def solution(mesh):

time: 68.3 us -> 66.4 us (0.972)
  local copies, waits for them, and re-layouts: 1.96 us -> 0.16 us
  blocking collectives: 58.3 us -> 57.6 us
    reshape x2 -> x1, local copies, waits for them, and re-layouts: 1.33 us -> 0.16 us  [per_device(): parcel = lax.all_to_all(parcel, 'visit', split_axis=0, concat_axis=0, til...]
    all_to_all x2, blocking collectives: 58.3 us -> 57.6 us  [the longest x1 44.7 us: per_device(): lax.all_to_all(parcel, 'visit', split_axis=0, concat_axis=0, tiled=True)]
    pallas_call x2 -> x3, Pallas kernels: 7.09 us -> 7.76 us  [the longest x1 4.89 us: warp_and_pack(): pl.pallas_call(warp_kernel, out_shape=jax.ShapeDtypeStruct((slots // 2, 2...]
where the time goes in v4:
time: 66.4 us; the launch traced here: 66.2 us
  blocking collectives  57.6 us (87%)
  Pallas kernels  7.76 us (12%)
    all_to_all x1, blocking collectives, per_device(): lax.all_to_all(parcel, 'visit', split_axis=0, concat_axis=0, tiled=True)  44.7 us
    all_to_all x1, blocking collectives, per_device(): lax.all_to_all(parts, 'tract', split_axis=0, concat_axis=0, tiled=True)  12.9 us
    pallas_call x1, Pallas kernels, warp_and_pack(): pl.pallas_call(warp_kernel, out_shape=jax.ShapeDtypeStruct((slots // 2, 2...  4.89 us
    pallas_call x1, Pallas kernels, place(): pl.pallas_call(place_kernel, out_shape=jax.ShapeDtypeStruct((tracts, PATC...  1.94 us

profile of v4, /device:TPU:1, one launch (start us, length us, event | category | flops | bytes accessed | tf_op | source)
XLA Modules:
  0.0 66.2 jit_solution(10679834213085100160)
XLA Ops:
  0.6 4.9 %warp_and_pack.1 = bf16[64,2,1664]{2,1,0:T(2,128)(2,1)} custom-call(bf16[32,6400]{1,0:T(8,128)(2,1)} %bitcast.11, bf16[32,96]{1,0:T(8,128)(2,1)} %bitcast.13, s32[1,32]{1,0:T(1,128)} %orders_ref.1, bf16[32,3200]{1,0:T(8,128)(2,1)} %bitcast.12, bf16[1,32]{1,0:T(2,128)(2,1)} %weights_ref.1, s32[2,32]{1,0:T(2,128)} %bitcast.15, s32[2,2,32]{2,1,0:T(2,128)} %bitcast.14, ...), custom_call_target="tpu_custom_call" | custom-call | tf_op jit(solution)/shard_map/warp_and_pack/pallas_call | solution.py:255
  5.5 44.7 %all_to_all.10 = bf16[64,2,1664]{2,1,0:T(2,128)(2,1)S(1)} all-to-all(bf16[64,2,1664]{2,1,0:T(2,128)(2,1)} %warp_and_pack.1), channel_id=1, replica_groups=mesh['tract'=8,'visit'=64] {'visit'}, dimensions={0} | all-to-all | bytes 851968 | tf_op jit(solution)/shard_map/all_to_all | solution.py:400
  50.2 0.2 reshape.7.parcel_ref
  50.4 1.9 %place_in_patch.1 = bf16[8,40,256]{2,1,0:T(8,128)(2,1)S(1)} custom-call(bf16[128,1664]{1,0:T(8,128)(2,1)S(1)} %reshape.7.parcel_ref), custom_call_target="tpu_custom_call" | custom-call | tf_op jit(solution)/shard_map/place_in_patch/pallas_call | solution.py:336
  52.3 12.9 %all_to_all.11.parts_ref = bf16[8,40,256]{2,1,0:T(8,128)(2,1)S(1)} all-to-all(bf16[8,40,256]{2,1,0:T(8,128)(2,1)S(1)} %place_in_patch.1), channel_id=1, replica_groups=mesh['tract'=8,'visit'=64] {'tract'}, dimensions={0} | all-to-all | bytes 327680 | tf_op jit(solution)/shard_map/all_to_all | solution.py:404
  65.3 0.9 %finish.1 = (f32[32,256]{1,0:T(8,128)}, f32[32,256]{1,0:T(8,128)}) custom-call(bf16[8,40,256]{2,1,0:T(8,128)(2,1)S(1)} %all_to_all.11.parts_ref), custom_call_target="tpu_custom_call" | custom-call | tf_op jit(solution)/shard_map/finish/pallas_call | solution.py:377

commit v5 on v4

--- a/solution.py
+++ b/solution.py
@@ -23,6 +23,17 @@
 SIGMAS = (0.7, 1.5, 3.0, 2.0)
 POWERS = (0, 0, 0, 1)
 COLUMN_AT = (0, 40, 80, 128)
+
+
+DEEP = 16
+START = (2, 8)
+
+
+def visit_order(count):
+    wide = count // DEEP
+    return [
+        (x + START[0]) % wide * DEEP + (z + START[1]) % DEEP for x in range(wide) for z in range(DEEP)
+    ]
 
 
 def constant_tables():
@@ -212,7 +223,11 @@
     slots, pairs = out_ref.shape[0] * out_ref.shape[1], TOP * blocks
     patch = jnp.concatenate([routes_ref[k : k + 1, :] for k in range(TOP)], axis=1)
     slot = lax.broadcasted_iota(jnp.int32, (slots, pairs), 0)
-    hit = jnp.where(patch == slot // 2, 1.0, 0.0)
+    place = slot // 2
+    member = ((place + DEEP * START[0]) & (-DEEP & (slots // 2 - 1))) | (
+        (place + START[1]) & (DEEP - 1)
+    )
+    hit = jnp.where(patch == member, 1.0, 0.0)
     before = lax.broadcasted_iota(jnp.int32, (pairs, pairs), 0)
     after = lax.broadcasted_iota(jnp.int32, (pairs, pairs), 1)
     rank = jnp.dot(
@@ -265,9 +280,9 @@
             *[pltpu.VMEM(array.shape, array.dtype) for array in kept],
             pltpu.SemaphoreType.DMA((len(kept),)),
         ],
-        compiler_params=pltpu.CompilerParams(vmem_limit_bytes=56 << 20),
+        compiler_params=pltpu.CompilerParams(vmem_limit_bytes=32 << 20),
         name="warp_and_pack",
-    )(*operands)
+    )(*[pltpu.with_memory_space_constraint(array, pltpu.HBM) for array in operands])
 
 
 def place_kernel(parcel_ref, out_ref, slot_rows, spread_left, spread_right, corner_x_wide):
@@ -398,7 +413,12 @@
         slot_count,
     )
     parcel = lax.all_to_all(
-        parcel, "visit", split_axis=0, concat_axis=0, tiled=True
+        parcel,
+        "visit",
+        split_axis=0,
+        concat_axis=0,
+        tiled=True,
+        axis_index_groups=[visit_order(visit_count)],
     ).reshape(slot_count, WIDTH)
     parts = place(parcel, tract_count)
     parts = lax.all_to_all(parts, "tract", split_axis=0, concat_axis=0, tiled=True)

time: 66.4 us -> 60.4 us (0.910)
  blocking collectives: 57.6 us -> 52.4 us
  Pallas kernels: 7.76 us -> 7 us
    all_to_all x1, blocking collectives: 44.7 us -> 41.1 us  [per_device(): lax.all_to_all(parcel, 'visit', split_axis=0, concat_axis=0, tiled=True,...]
    all_to_all x1, blocking collectives: 12.9 us -> 11.3 us  [per_device(): lax.all_to_all(parts, 'tract', split_axis=0, concat_axis=0, tiled=True)]
    pallas_call x1, Pallas kernels: 4.89 us -> 4.12 us  [warp_and_pack(): pl.pallas_call(warp_kernel, out_shape=jax.ShapeDtypeStruct((slots // 2, 2...]
where the time goes in v5:
time: 60.4 us; the launch traced here: 60.2 us
  blocking collectives  52.4 us (87%)
  Pallas kernels  7 us (12%)
  between operations  0.65 us (1%)
    all_to_all x1, blocking collectives, per_device(): lax.all_to_all(parcel, 'visit', split_axis=0, concat_axis=0, tiled=True,...  41.1 us
    all_to_all x1, blocking collectives, per_device(): lax.all_to_all(parts, 'tract', split_axis=0, concat_axis=0, tiled=True)  11.3 us
    pallas_call x1, Pallas kernels, warp_and_pack(): pl.pallas_call(warp_kernel, out_shape=jax.ShapeDtypeStruct((slots // 2, 2...  4.12 us
    pallas_call x1, Pallas kernels, place(): pl.pallas_call(place_kernel, out_shape=jax.ShapeDtypeStruct((tracts, PATC...  1.94 us

profile of v5, /device:TPU:1, one launch (start us, length us, event | category | flops | bytes accessed | tf_op | source)
XLA Modules:
  0.0 60.2 jit_solution(3365173881189839296)
XLA Ops:
  0.6 4.1 %warp_and_pack.1 = bf16[64,2,1664]{2,1,0:T(2,128)(2,1)S(1)} custom-call(bf16[32,6400]{1,0:T(8,128)(2,1)} %bitcast.11, bf16[32,96]{1,0:T(8,128)(2,1)} %bitcast.13, s32[1,32]{1,0:T(1,128)} %orders_ref.1, bf16[32,3200]{1,0:T(8,128)(2,1)} %bitcast.12, bf16[1,32]{1,0:T(2,128)(2,1)} %weights_ref.1, s32[2,32]{1,0:T(2,128)} %bitcast.15, s32[2,2,32]{2,1,0:T(2,128)} %bitcast.14, ...), custom_call_target="tpu_custom_call" | custom-call | tf_op jit(solution)/shard_map/warp_and_pack/pallas_call | solution.py:270
  4.8 41.1 %all_to_all.10 = bf16[64,2,1664]{2,1,0:T(2,128)(2,1)S(1)} all-to-all(bf16[64,2,1664]{2,1,0:T(2,128)(2,1)S(1)} %warp_and_pack.1), channel_id=1, replica_groups={{40,41,42,43,44,45,46,47,32,33,34,35,36,37,38,39,56,57,58,59,60,61,62,6..., dimensions={0} | all-to-all | bytes 851968 | tf_op jit(solution)/shard_map/all_to_all | solution.py:415
  45.8 0.2 reshape.7.parcel_ref
  46.0 1.9 %place_in_patch.1 = bf16[8,40,256]{2,1,0:T(8,128)(2,1)S(1)} custom-call(bf16[128,1664]{1,0:T(8,128)(2,1)S(1)} %reshape.7.parcel_ref), custom_call_target="tpu_custom_call" | custom-call | tf_op jit(solution)/shard_map/place_in_patch/pallas_call | solution.py:351
  47.9 11.3 %all_to_all.11.parts_ref = bf16[8,40,256]{2,1,0:T(8,128)(2,1)S(1)} all-to-all(bf16[8,40,256]{2,1,0:T(8,128)(2,1)S(1)} %place_in_patch.1), channel_id=1, replica_groups=mesh['tract'=8,'visit'=64] {'tract'}, dimensions={0} | all-to-all | bytes 327680 | tf_op jit(solution)/shard_map/all_to_all | solution.py:424
  59.2 0.9 %finish.1 = (f32[32,256]{1,0:T(8,128)}, f32[32,256]{1,0:T(8,128)}) custom-call(bf16[8,40,256]{2,1,0:T(8,128)(2,1)S(1)} %all_to_all.11.parts_ref), custom_call_target="tpu_custom_call" | custom-call | tf_op jit(solution)/shard_map/finish/pallas_call | solution.py:392

commit v6 on v5

--- a/solution.py
+++ b/solution.py
@@ -27,6 +27,7 @@
 
 DEEP = 16
 START = (2, 8)
+FIRST = 5
 
 
 def visit_order(count):
@@ -34,6 +35,10 @@
     return [
         (x + START[0]) % wide * DEEP + (z + START[1]) % DEEP for x in range(wide) for z in range(DEEP)
     ]
+
+
+def tract_order(count):
+    return [(t + FIRST) % count for t in range(count)]
 
 
 def constant_tables():
@@ -338,11 +343,11 @@
         ).astype(bf16)
         flux += jnp.dot(row, across, preferred_element_type=f32)
     blank = jnp.zeros((6, PATCH), f32)
-    for t in range(tracts):
+    for place, t in enumerate(tract_order(tracts)):
         corners = jnp.concatenate([corner_y - float(rows * t), corner_x_row], axis=1)
         weights = jnp.concatenate([weight, jnp.zeros_like(weight)], axis=1)
         parts = [flux[rows * t : rows * (t + 1), :], corners, weights, blank]
-        out_ref[t] = jnp.concatenate(parts, axis=0).astype(bf16)
+        out_ref[place] = jnp.concatenate(parts, axis=0).astype(bf16)
 
 
 def place(parcel, tracts):
@@ -421,7 +426,14 @@
         axis_index_groups=[visit_order(visit_count)],
     ).reshape(slot_count, WIDTH)
     parts = place(parcel, tract_count)
-    parts = lax.all_to_all(parts, "tract", split_axis=0, concat_axis=0, tiled=True)
+    parts = lax.all_to_all(
+        parts,
+        "tract",
+        split_axis=0,
+        concat_axis=0,
+        tiled=True,
+        axis_index_groups=[tract_order(tract_count)],
+    )
     flux, cover = finish(parts, tract_count)
     return (flux[None], cover[None])
 

time: 60.4 us -> 58.1 us (0.962)
  blocking collectives: 52.4 us -> 50.1 us
    all_to_all x1, blocking collectives: 11.3 us -> 9.04 us  [per_device(): lax.all_to_all(parts, 'tract', split_axis=0, concat_axis=0, tiled=True, a...]
where the time goes in v6:
time: 58.1 us; the launch traced here: 57.9 us
  blocking collectives  50.1 us (86%)
  Pallas kernels  7 us (12%)
  between operations  0.65 us (1%)
    all_to_all x1, blocking collectives, per_device(): lax.all_to_all(parcel, 'visit', split_axis=0, concat_axis=0, tiled=True,...  41.1 us
    all_to_all x1, blocking collectives, per_device(): lax.all_to_all(parts, 'tract', split_axis=0, concat_axis=0, tiled=True, a...  9.04 us
    pallas_call x1, Pallas kernels, warp_and_pack(): pl.pallas_call(warp_kernel, out_shape=jax.ShapeDtypeStruct((slots // 2, 2...  4.12 us
    pallas_call x1, Pallas kernels, place(): pl.pallas_call(place_kernel, out_shape=jax.ShapeDtypeStruct((tracts, PATC...  1.94 us

profile of v6, /device:TPU:1, one launch (start us, length us, event | category | flops | bytes accessed | tf_op | source)
XLA Modules:
  0.0 57.9 jit_solution(2973556404008370489)
XLA Ops:
  0.6 4.1 %warp_and_pack.1 = bf16[64,2,1664]{2,1,0:T(2,128)(2,1)S(1)} custom-call(bf16[32,6400]{1,0:T(8,128)(2,1)} %bitcast.11, bf16[32,96]{1,0:T(8,128)(2,1)} %bitcast.13, s32[1,32]{1,0:T(1,128)} %orders_ref.1, bf16[32,3200]{1,0:T(8,128)(2,1)} %bitcast.12, bf16[1,32]{1,0:T(2,128)(2,1)} %weights_ref.1, s32[2,32]{1,0:T(2,128)} %bitcast.15, s32[2,2,32]{2,1,0:T(2,128)} %bitcast.14, ...), custom_call_target="tpu_custom_call" | custom-call | tf_op jit(solution)/shard_map/warp_and_pack/pallas_call | solution.py:275
  4.8 41.1 %all_to_all.10 = bf16[64,2,1664]{2,1,0:T(2,128)(2,1)S(1)} all-to-all(bf16[64,2,1664]{2,1,0:T(2,128)(2,1)S(1)} %warp_and_pack.1), channel_id=1, replica_groups={{40,41,42,43,44,45,46,47,32,33,34,35,36,37,38,39,56,57,58,59,60,61,62,6..., dimensions={0} | all-to-all | bytes 851968 | tf_op jit(solution)/shard_map/all_to_all | solution.py:420
  45.8 0.2 reshape.7.parcel_ref
  46.0 1.9 %place_in_patch.1 = bf16[8,40,256]{2,1,0:T(8,128)(2,1)S(1)} custom-call(bf16[128,1664]{1,0:T(8,128)(2,1)S(1)} %reshape.7.parcel_ref), custom_call_target="tpu_custom_call" | custom-call | tf_op jit(solution)/shard_map/place_in_patch/pallas_call | solution.py:356
  47.9 9.0 %all_to_all.11.parts_ref = bf16[8,40,256]{2,1,0:T(8,128)(2,1)S(1)} all-to-all(bf16[8,40,256]{2,1,0:T(8,128)(2,1)S(1)} %place_in_patch.1), channel_id=1, replica_groups={{320,384,448,0,64,128,192,256},{321,385,449,1,65,129,193,257},{322,386,..., dimensions={0} | all-to-all | bytes 327680 | tf_op jit(solution)/shard_map/all_to_all | solution.py:429
  57.0 0.9 %finish.1 = (f32[32,256]{1,0:T(8,128)}, f32[32,256]{1,0:T(8,128)}) custom-call(bf16[8,40,256]{2,1,0:T(8,128)(2,1)S(1)} %all_to_all.11.parts_ref), custom_call_target="tpu_custom_call" | custom-call | tf_op jit(solution)/shard_map/finish/pallas_call | solution.py:397

commit v7 on v6

--- a/solution.py
+++ b/solution.py
@@ -26,7 +26,7 @@
 
 
 DEEP = 16
-START = (2, 8)
+START = (2, 9)
 FIRST = 5
 
 
@@ -277,10 +277,10 @@
         out_shape=jax.ShapeDtypeStruct((slots // 2, 2, WIDTH), jnp.bfloat16),
         in_specs=[pl.BlockSpec(memory_space=pl.ANY)] * len(operands),
         scratch_shapes=[
-            pltpu.VMEM((blocks * (BLKIN + 1), LANES), f32),
-            pltpu.VMEM((blocks * (2 * BLK + 1), LANES), f32),
+            pltpu.VMEM(((blocks + 1) * (BLKIN + 1), LANES), f32),
+            pltpu.VMEM(((blocks + 1) * (2 * BLK + 1), LANES), f32),
             pltpu.VMEM((blocks * 4, 3 * 2 * LANES), f32),
-            pltpu.VMEM((blocks * (BLK + 1), LANES), f32),
+            pltpu.VMEM(((blocks + 1) * (BLK + 1), LANES), f32),
             pltpu.VMEM((blocks, WIDTH), f32),
             *[pltpu.VMEM(array.shape, array.dtype) for array in kept],
             pltpu.SemaphoreType.DMA((len(kept),)),
@@ -357,9 +357,9 @@
         place_kernel,
         out_shape=jax.ShapeDtypeStruct((tracts, PATCH // tracts + 8, PATCH), jnp.bfloat16),
         scratch_shapes=[
-            pltpu.VMEM((slots * (BLK + 1), LANES), f32),
-            pltpu.VMEM(((slots + 1) * BLK, LANES), f32),
-            pltpu.VMEM(((slots + 1) * BLK, LANES), f32),
+            pltpu.VMEM(((slots + 1) * (BLK + 1), LANES), f32),
+            pltpu.VMEM(((slots + 1) * (BLK + 1), LANES), f32),
+            pltpu.VMEM(((slots + 1) * (BLK + 1), LANES), f32),
             pltpu.VMEM((slots, PATCH), f32),
         ],
         compiler_params=pltpu.CompilerParams(vmem_limit_bytes=24 << 20),

time: 58.1 us -> 57.8 us (level)
  no operation moved by 1% of the time
where the time goes in v7:
time: 57.8 us; the launch traced here: 57.6 us
  blocking collectives  49.8 us (86%)
  Pallas kernels  7 us (12%)
  between operations  0.65 us (1%)
    all_to_all x1, blocking collectives, per_device(): lax.all_to_all(parcel, 'visit', split_axis=0, concat_axis=0, tiled=True,...  41.3 us
    all_to_all x1, blocking collectives, per_device(): lax.all_to_all(parts, 'tract', split_axis=0, concat_axis=0, tiled=True, a...  8.53 us
    pallas_call x1, Pallas kernels, warp_and_pack(): pl.pallas_call(warp_kernel, out_shape=jax.ShapeDtypeStruct((slots // 2, 2...  4.12 us
    pallas_call x1, Pallas kernels, place(): pl.pallas_call(place_kernel, out_shape=jax.ShapeDtypeStruct((tracts, PATC...  1.94 us

profile of v7, /device:TPU:1, one launch (start us, length us, event | category | flops | bytes accessed | tf_op | source)
XLA Modules:
  0.0 57.6 jit_solution(1880405572871358984)
XLA Ops:
  0.6 4.1 %warp_and_pack.1 = bf16[64,2,1664]{2,1,0:T(2,128)(2,1)S(1)} custom-call(bf16[32,6400]{1,0:T(8,128)(2,1)} %bitcast.11, bf16[32,96]{1,0:T(8,128)(2,1)} %bitcast.13, s32[1,32]{1,0:T(1,128)} %orders_ref.1, bf16[32,3200]{1,0:T(8,128)(2,1)} %bitcast.12, bf16[1,32]{1,0:T(2,128)(2,1)} %weights_ref.1, s32[2,32]{1,0:T(2,128)} %bitcast.15, s32[2,2,32]{2,1,0:T(2,128)} %bitcast.14, ...), custom_call_target="tpu_custom_call" | custom-call | tf_op jit(solution)/shard_map/warp_and_pack/pallas_call | solution.py:275
  4.8 41.3 %all_to_all.10 = bf16[64,2,1664]{2,1,0:T(2,128)(2,1)S(1)} all-to-all(bf16[64,2,1664]{2,1,0:T(2,128)(2,1)S(1)} %warp_and_pack.1), channel_id=1, replica_groups={{41,42,43,44,45,46,47,32,33,34,35,36,37,38,39,40,57,58,59,60,61,62,63,4..., dimensions={0} | all-to-all | bytes 851968 | tf_op jit(solution)/shard_map/all_to_all | solution.py:420
  46.0 0.2 reshape.7.parcel_ref
  46.2 1.9 %place_in_patch.1 = bf16[8,40,256]{2,1,0:T(8,128)(2,1)S(1)} custom-call(bf16[128,1664]{1,0:T(8,128)(2,1)S(1)} %reshape.7.parcel_ref), custom_call_target="tpu_custom_call" | custom-call | tf_op jit(solution)/shard_map/place_in_patch/pallas_call | solution.py:356
  48.2 8.5 %all_to_all.11.parts_ref = bf16[8,40,256]{2,1,0:T(8,128)(2,1)S(1)} all-to-all(bf16[8,40,256]{2,1,0:T(8,128)(2,1)S(1)} %place_in_patch.1), channel_id=1, replica_groups={{320,384,448,0,64,128,192,256},{321,385,449,1,65,129,193,257},{322,386,..., dimensions={0} | all-to-all | bytes 327680 | tf_op jit(solution)/shard_map/all_to_all | solution.py:429
  56.7 0.9 %finish.1 = (f32[32,256]{1,0:T(8,128)}, f32[32,256]{1,0:T(8,128)}) custom-call(bf16[8,40,256]{2,1,0:T(8,128)(2,1)S(1)} %all_to_all.11.parts_ref), custom_call_target="tpu_custom_call" | custom-call | tf_op jit(solution)/shard_map/finish/pallas_call | solution.py:397

commit v8 on v7

--- a/solution.py
+++ b/solution.py
@@ -225,7 +225,7 @@
         flat[:, BLK * i : BLK * (i + 1)] = warped_rows[pl.ds(i, blocks, stride=BLK + 1), 0:BLK]
     pixels = flat[...].astype(bf16)
 
-    slots, pairs = out_ref.shape[0] * out_ref.shape[1], TOP * blocks
+    slots, pairs = out_ref.shape[0], TOP * blocks
     patch = jnp.concatenate([routes_ref[k : k + 1, :] for k in range(TOP)], axis=1)
     slot = lax.broadcasted_iota(jnp.int32, (slots, pairs), 0)
     place = slot // 2
@@ -255,7 +255,7 @@
     ).astype(bf16)
     tail = lax.dot_general(pick, extras, (((1,), (1,)), ((), ())), preferred_element_type=f32)
     packed = jnp.concatenate([packed[:, : 12 * LANES], packed[:, 12 * LANES :] + tail], axis=1)
-    out_ref[...] = packed.astype(bf16).reshape(out_ref.shape)
+    out_ref[...] = packed.astype(bf16)
 
 
 def warp_and_pack(images, coefficients, orders, resample, weights, routes, offsets, slots):
@@ -274,7 +274,7 @@
     kept = [operands[n] for n in (0, 3, 1, 2, 4, 5, 6, 7)]
     return pl.pallas_call(
         warp_kernel,
-        out_shape=jax.ShapeDtypeStruct((slots // 2, 2, WIDTH), jnp.bfloat16),
+        out_shape=jax.ShapeDtypeStruct((slots, WIDTH), jnp.bfloat16),
         in_specs=[pl.BlockSpec(memory_space=pl.ANY)] * len(operands),
         scratch_shapes=[
             pltpu.VMEM(((blocks + 1) * (BLKIN + 1), LANES), f32),
@@ -314,7 +314,7 @@
         lax.broadcasted_iota(jnp.int32, (BLK, PATCH), 1)
         - lax.broadcasted_iota(jnp.int32, (BLK, PATCH), 0)
     ).astype(f32)
-    batch = 16
+    batch = 32
     for first in range(0, slots, batch):
         placed = []
         for s in range(first, first + batch):
@@ -424,7 +424,7 @@
         concat_axis=0,
         tiled=True,
         axis_index_groups=[visit_order(visit_count)],
-    ).reshape(slot_count, WIDTH)
+    )
     parts = place(parcel, tract_count)
     parts = lax.all_to_all(
         parts,

time: 57.8 us -> 58 us (level)
  no operation moved by 1% of the time
where the time goes in v8:
time: 58 us; the launch traced here: 57.8 us
  blocking collectives  49.8 us (86%)
  Pallas kernels  6.99 us (12%)
  between operations  0.66 us (1%)
    all_to_all x1, blocking collectives, per_device(): lax.all_to_all(parcel, 'visit', split_axis=0, concat_axis=0, tiled=True,...  41.3 us
    all_to_all x1, blocking collectives, per_device(): lax.all_to_all(parts, 'tract', split_axis=0, concat_axis=0, tiled=True, a...  8.54 us
    pallas_call x1, Pallas kernels, warp_and_pack(): pl.pallas_call(warp_kernel, out_shape=jax.ShapeDtypeStruct((slots, WIDTH)...  4.11 us
    pallas_call x1, Pallas kernels, place(): pl.pallas_call(place_kernel, out_shape=jax.ShapeDtypeStruct((tracts, PATC...  1.94 us

profile of v8, /device:TPU:1, one launch (start us, length us, event | category | flops | bytes accessed | tf_op | source)
XLA Modules:
  0.0 57.8 jit_solution(17683868043693059835)
XLA Ops:
  0.6 4.1 %warp_and_pack.1 = bf16[128,1664]{1,0:T(8,128)(2,1)S(1)} custom-call(bf16[32,6400]{1,0:T(8,128)(2,1)} %bitcast.11, bf16[32,96]{1,0:T(8,128)(2,1)} %bitcast.13, s32[1,32]{1,0:T(1,128)} %orders_ref.1, bf16[32,3200]{1,0:T(8,128)(2,1)} %bitcast.12, bf16[1,32]{1,0:T(2,128)(2,1)} %weights_ref.1, s32[2,32]{1,0:T(2,128)} %bitcast.15, s32[2,2,32]{2,1,0:T(2,128)} %bitcast.14, ...), custom_call_target="tpu_custom_call" | custom-call | tf_op jit(solution)/shard_map/warp_and_pack/pallas_call | solution.py:275
  4.8 0.2 all_to_all.10
  4.9 41.3 %all_to_all.16 = bf16[64,2,1664]{2,1,0:T(2,128)(2,1)S(1)} all-to-all(bf16[64,2,1664]{2,1,0:T(2,128)(2,1)S(1)} %all_to_all.10), channel_id=1, replica_groups={{41,42,43,44,45,46,47,32,33,34,35,36,37,38,39,40,57,58,59,60,61,62,63,4..., dimensions={0} | all-to-all | bytes 851968 | tf_op jit(solution)/shard_map/all_to_all | solution.py:420
  46.2 0.2 all_to_all.12.parcel_ref
  46.4 1.9 %place_in_patch.1 = bf16[8,40,256]{2,1,0:T(8,128)(2,1)S(1)} custom-call(bf16[128,1664]{1,0:T(8,128)(2,1)S(1)} %all_to_all.12.parcel_ref), custom_call_target="tpu_custom_call" | custom-call | tf_op jit(solution)/shard_map/place_in_patch/pallas_call | solution.py:356
  48.3 8.5 %all_to_all.17.parts_ref = bf16[8,40,256]{2,1,0:T(8,128)(2,1)S(1)} all-to-all(bf16[8,40,256]{2,1,0:T(8,128)(2,1)S(1)} %place_in_patch.1), channel_id=1, replica_groups={{320,384,448,0,64,128,192,256},{321,385,449,1,65,129,193,257},{322,386,..., dimensions={0} | all-to-all | bytes 327680 | tf_op jit(solution)/shard_map/all_to_all | solution.py:429
  56.9 0.9 %finish.1 = (f32[32,256]{1,0:T(8,128)}, f32[32,256]{1,0:T(8,128)}) custom-call(bf16[8,40,256]{2,1,0:T(8,128)(2,1)S(1)} %all_to_all.17.parts_ref), custom_call_target="tpu_custom_call" | custom-call | tf_op jit(solution)/shard_map/finish/pallas_call | solution.py:397

commit v9 on v7

--- a/solution.py
+++ b/solution.py
@@ -290,7 +290,7 @@
     )(*[pltpu.with_memory_space_constraint(array, pltpu.HBM) for array in operands])
 
 
-def place_kernel(parcel_ref, out_ref, slot_rows, spread_left, spread_right, corner_x_wide):
+def place_kernel(parcel_ref, out_ref, slot_rows, spread_left, spread_right, corner_x_wide, row_hits):
     f32, bf16 = jnp.float32, jnp.bfloat16
     slots = parcel_ref.shape[0]
     tracts, rows = out_ref.shape[0], PATCH // out_ref.shape[0]
@@ -325,12 +325,13 @@
             spread_left[pl.ds(s, BLK, stride=pitch), :] = placed[s - first][:, :LANES]
             spread_right[pl.ds(s, BLK, stride=pitch), :] = placed[s - first][:, LANES:]
 
-    above = lax.broadcasted_iota(jnp.int32, (PATCH, slots), 0).astype(f32) - corner_y
+    shifted = lax.broadcasted_iota(jnp.int32, (PATCH + BLK, slots), 0).astype(f32) - corner_y
+    row_hits[...] = jnp.where(shifted == float(BLK), weight, 0.0)
     flux = jnp.zeros((PATCH, PATCH), f32)
     depth = 2
     for i in range(0, BLK, depth):
         row = jnp.concatenate(
-            [jnp.where(above == float(i + n), weight, 0.0).astype(bf16) for n in range(depth)], axis=1
+            [row_hits[BLK - i - n : BLK - i - n + PATCH, :].astype(bf16) for n in range(depth)], axis=1
         )
         across = jnp.concatenate(
             [
@@ -361,6 +362,7 @@
             pltpu.VMEM(((slots + 1) * (BLK + 1), LANES), f32),
             pltpu.VMEM(((slots + 1) * (BLK + 1), LANES), f32),
             pltpu.VMEM((slots, PATCH), f32),
+            pltpu.VMEM((PATCH + BLK, slots), f32),
         ],
         compiler_params=pltpu.CompilerParams(vmem_limit_bytes=24 << 20),
         name="place_in_patch",

time: 57.8 us -> 57.8 us (level)
  no operation moved by 1% of the time
where the time goes in v9:
time: 57.8 us; the launch traced here: 57.6 us
  blocking collectives  49.8 us (86%)
  Pallas kernels  7 us (12%)
  between operations  0.65 us (1%)
    all_to_all x1, blocking collectives, per_device(): lax.all_to_all(parcel, 'visit', split_axis=0, concat_axis=0, tiled=True,...  41.3 us
    all_to_all x1, blocking collectives, per_device(): lax.all_to_all(parts, 'tract', split_axis=0, concat_axis=0, tiled=True, a...  8.53 us
    pallas_call x1, Pallas kernels, warp_and_pack(): pl.pallas_call(warp_kernel, out_shape=jax.ShapeDtypeStruct((slots // 2, 2...  4.12 us
    pallas_call x1, Pallas kernels, place(): pl.pallas_call(place_kernel, out_shape=jax.ShapeDtypeStruct((tracts, PATC...  1.95 us

profile of v9, /device:TPU:1, one launch (start us, length us, event | category | flops | bytes accessed | tf_op | source)
XLA Modules:
  0.0 57.6 jit_solution(7992012225061725469)
XLA Ops:
  0.6 4.1 %warp_and_pack.1 = bf16[64,2,1664]{2,1,0:T(2,128)(2,1)S(1)} custom-call(bf16[32,6400]{1,0:T(8,128)(2,1)} %bitcast.11, bf16[32,96]{1,0:T(8,128)(2,1)} %bitcast.13, s32[1,32]{1,0:T(1,128)} %orders_ref.1, bf16[32,3200]{1,0:T(8,128)(2,1)} %bitcast.12, bf16[1,32]{1,0:T(2,128)(2,1)} %weights_ref.1, s32[2,32]{1,0:T(2,128)} %bitcast.15, s32[2,2,32]{2,1,0:T(2,128)} %bitcast.14, ...), custom_call_target="tpu_custom_call" | custom-call | tf_op jit(solution)/shard_map/warp_and_pack/pallas_call | solution.py:275
  4.8 41.3 %all_to_all.10 = bf16[64,2,1664]{2,1,0:T(2,128)(2,1)S(1)} all-to-all(bf16[64,2,1664]{2,1,0:T(2,128)(2,1)S(1)} %warp_and_pack.1), channel_id=1, replica_groups={{41,42,43,44,45,46,47,32,33,34,35,36,37,38,39,40,57,58,59,60,61,62,63,4..., dimensions={0} | all-to-all | bytes 851968 | tf_op jit(solution)/shard_map/all_to_all | solution.py:422
  46.0 0.2 reshape.7.parcel_ref
  46.2 1.9 %place_in_patch.1 = bf16[8,40,256]{2,1,0:T(8,128)(2,1)S(1)} custom-call(bf16[128,1664]{1,0:T(8,128)(2,1)S(1)} %reshape.7.parcel_ref), custom_call_target="tpu_custom_call" | custom-call | tf_op jit(solution)/shard_map/place_in_patch/pallas_call | solution.py:357
  48.2 8.5 %all_to_all.11.parts_ref = bf16[8,40,256]{2,1,0:T(8,128)(2,1)S(1)} all-to-all(bf16[8,40,256]{2,1,0:T(8,128)(2,1)S(1)} %place_in_patch.1), channel_id=1, replica_groups={{320,384,448,0,64,128,192,256},{321,385,449,1,65,129,193,257},{322,386,..., dimensions={0} | all-to-all | bytes 327680 | tf_op jit(solution)/shard_map/all_to_all | solution.py:431
  56.7 0.9 %finish.1 = (f32[32,256]{1,0:T(8,128)}, f32[32,256]{1,0:T(8,128)}) custom-call(bf16[8,40,256]{2,1,0:T(8,128)(2,1)S(1)} %all_to_all.11.parts_ref), custom_call_target="tpu_custom_call" | custom-call | tf_op jit(solution)/shard_map/finish/pallas_call | solution.py:399
